TPU v7x, 512 devices: a whole 4x4x16 slice. The times are simulated.
512 devices in a mesh: expert: 64 (over x, y, z_hi), fsdp: 8 (over z_lo, core).
Axes of the slice: x: 4, y: 4, z: 16 (z_hi: 4, z_lo: 4; z = z_hi * 4 + z_lo), core: 2. Of those that a mesh axis runs over, the one named last changes fastest.
Arguments:
- tokens: bfloat16 [8192, 4096], P('expert', 'fsdp'), may hold values from -6 to 6
- routes: int32 [8192, 8], P('expert'), may hold values from 0 to 63, all different within a row; in each aligned block of 128 rows (0 to 127, 128 to 255, ...) at most 32 rows name the same one
- hidden_grad: bfloat16 [8192, 8, 768], P('expert', None, 'fsdp'), may hold values from -6 to 6
- gate_base: bfloat16 [4096, 768], P('fsdp'), may hold values from -0.09375 to 0.09375
- up_base: bfloat16 [4096, 768], P('fsdp'), may hold values from -0.09375 to 0.09375
- gate_left: bfloat16 [64, 4096, 128], P('expert', 'fsdp'), may hold values from -0.09375 to 0.09375
- up_left: bfloat16 [64, 4096, 128], P('expert', 'fsdp'), may hold values from -0.09375 to 0.09375
- gate_right: bfloat16 [64, 128, 768], P('expert', None, 'fsdp'), may hold values from -0.5 to 0.5
- up_right: bfloat16 [64, 128, 768], P('expert', None, 'fsdp'), may hold values from -0.5 to 0.5
Outputs:
- tokens_grad: bfloat16 [8192, 4096], P('expert', 'fsdp')
- gate_base_grad: float32 [4096, 768], P(('fsdp', 'expert'))
- up_base_grad: float32 [4096, 768], P(('fsdp', 'expert'))
- gate_left_grad: float32 [64, 4096, 128], P('expert', 'fsdp')
- up_left_grad: float32 [64, 4096, 128], P('expert', 'fsdp')
- gate_right_grad: float32 [64, 128, 768], P('expert', None, 'fsdp')
- up_right_grad: float32 [64, 128, 768], P('expert', None, 'fsdp')
Inputs may be any that keep to these rules, and one draw needn't show every extreme that they name: `routes`: each row names 8 different experts. Within the tokens of one index of expert, no expert is named more than 32 times, a bound that some block reaches.
All inputs are finite; a program needn't handle non-finite values.
Results may differ from a plain program's by a relative error of at most 0.0069.
Values may be sent and summed in bfloat16 or wider, within the bound.
A program may use at most 64 MiB of HBM per device.

v0:
```python
import jax
import jax.numpy as jnp
from jax import lax
from jax.sharding import PartitionSpec as P


def contract_last(left_mat, right_mat):
    return lax.dot_general(
        left_mat, right_mat, (((1,), (1,)), ((), ())), preferred_element_type=jnp.float32
    )


def contract_first(left_mat, right_mat):
    return lax.dot_general(
        left_mat, right_mat, (((0,), (0,)), ((), ())), preferred_element_type=jnp.float32
    )


def local(
    tokens, routes, hidden_grad, gate_base, up_base, gate_left, up_left, gate_right, up_right
):
    groups = lax.axis_size("expert")
    tok_rows, topk_count = routes.shape
    experts_all = groups * gate_left.shape[0]
    capacity = max(2, 2 * tok_rows * topk_count // experts_all)
    copies = tok_rows * topk_count
    flat_route = routes.reshape(-1)
    onehot_table = (
        flat_route[:, None] == jnp.arange(experts_all, dtype=jnp.int32)[None, :]
    ).astype(jnp.int32)
    earlier = jnp.cumsum(onehot_table, axis=0) - onehot_table
    place = jnp.sum(earlier * onehot_table, axis=1)
    slot_index = flat_route * capacity + place
    owner = (
        jnp.full((experts_all * capacity,), -1, jnp.int32)
        .at[slot_index]
        .set(jnp.arange(copies, dtype=jnp.int32))
    )
    filled = (owner >= 0)[:, None]
    safe_copy = jnp.where(owner >= 0, owner, 0)
    safe_token = safe_copy // topk_count
    zero_half = jnp.zeros((), jnp.bfloat16)

    def to_slots(source, index):
        return jnp.where(filled, source[index], zero_half).reshape(experts_all, capacity, -1)

    send_rows = to_slots(tokens, safe_token)
    send_hidden = to_slots(hidden_grad.reshape(copies, -1), safe_copy)
    part_gate = jnp.dot(tokens, gate_base, preferred_element_type=jnp.float32)
    part_up = jnp.dot(tokens, up_base, preferred_element_type=jnp.float32)
    gate_share = lax.psum_scatter(part_gate, "fsdp", scatter_dimension=1, tiled=True)
    up_share = lax.psum_scatter(part_up, "fsdp", scatter_dimension=1, tiled=True)
    gate_act = gate_share.astype(jnp.bfloat16)
    up_act = up_share.astype(jnp.bfloat16)
    got_rows, got_gate, got_up, got_hidden = (
        lax.all_to_all(send_rows, "expert", split_axis=0, concat_axis=0, tiled=True),
        lax.all_to_all(
            to_slots(gate_act, safe_token), "expert", split_axis=0, concat_axis=0, tiled=True
        ),
        lax.all_to_all(
            to_slots(up_act, safe_token), "expert", split_axis=0, concat_axis=0, tiled=True
        ),
        lax.all_to_all(send_hidden, "expert", split_axis=0, concat_axis=0, tiled=True),
    )
    slots = got_rows.shape[0] * got_rows.shape[1]
    x_rows = got_rows.reshape(slots, -1)
    gate_low, up_low = lax.psum(
        (
            jnp.dot(x_rows, gate_left[0], preferred_element_type=jnp.float32),
            jnp.dot(x_rows, up_left[0], preferred_element_type=jnp.float32),
        ),
        "fsdp",
    )
    gate_low = gate_low.astype(jnp.bfloat16)
    up_low = up_low.astype(jnp.bfloat16)
    gate_pre = got_gate.reshape(slots, -1).astype(jnp.float32) + jnp.dot(
        gate_low, gate_right[0], preferred_element_type=jnp.float32
    )
    up_pre = got_up.reshape(slots, -1).astype(jnp.float32) + jnp.dot(
        up_low, up_right[0], preferred_element_type=jnp.float32
    )
    sigma = jax.nn.sigmoid(gate_pre)
    hidden_f = got_hidden.reshape(slots, -1).astype(jnp.float32)
    d_gate = (hidden_f * up_pre * sigma * (1.0 + gate_pre * (1.0 - sigma))).astype(jnp.bfloat16)
    d_up = (hidden_f * gate_pre * sigma).astype(jnp.bfloat16)
    gate_right_grad = contract_first(gate_low, d_gate)[None]
    up_right_grad = contract_first(up_low, d_up)[None]
    gate_back = d_gate.reshape(groups, capacity, -1)
    up_back = d_up.reshape(groups, capacity, -1)
    d_gate_low, d_up_low = lax.psum(
        (contract_last(d_gate, gate_right[0]), contract_last(d_up, up_right[0])), "fsdp"
    )
    d_gate_low = d_gate_low.astype(jnp.bfloat16)
    d_up_low = d_up_low.astype(jnp.bfloat16)
    left_gate = contract_first(x_rows, d_gate_low)[None]
    left_up = contract_first(x_rows, d_up_low)[None]
    delta_dx = (
        contract_last(d_gate_low, gate_left[0]) + contract_last(d_up_low, up_left[0])
    ).astype(jnp.bfloat16)
    delta_send = delta_dx.reshape(groups, capacity, -1)
    back_delta, back_gate, back_up = (
        lax.all_to_all(delta_send, "expert", split_axis=0, concat_axis=0, tiled=True),
        lax.all_to_all(gate_back, "expert", split_axis=0, concat_axis=0, tiled=True),
        lax.all_to_all(up_back, "expert", split_axis=0, concat_axis=0, tiled=True),
    )

    def token_totals(back):
        picked = back.reshape(experts_all * capacity, -1)[slot_index]
        return jnp.sum(picked.reshape(tok_rows, topk_count, -1).astype(jnp.float32), axis=1)

    gate_sum = token_totals(back_gate).astype(jnp.bfloat16)
    up_sum = token_totals(back_up).astype(jnp.bfloat16)
    gate_full, up_full = (
        lax.all_gather(gate_sum, "fsdp", axis=1, tiled=True),
        lax.all_gather(up_sum, "fsdp", axis=1, tiled=True),
    )
    delta_total = token_totals(back_delta)
    tokens_grad = (
        delta_total + contract_last(gate_full, gate_base) + contract_last(up_full, up_base)
    ).astype(jnp.bfloat16)
    gate_base_grad, up_base_grad = (
        lax.psum_scatter(
            contract_first(tokens, gate_full), "expert", scatter_dimension=0, tiled=True
        ),
        lax.psum_scatter(
            contract_first(tokens, up_full), "expert", scatter_dimension=0, tiled=True
        ),
    )
    return (
        tokens_grad,
        gate_base_grad,
        up_base_grad,
        left_gate,
        left_up,
        gate_right_grad,
        up_right_grad,
    )


def solution(mesh):
    return jax.shard_map(
        local,
        mesh=mesh,
        in_specs=(
            P("expert", "fsdp"),
            P("expert", None),
            P("expert", None, "fsdp"),
            P("fsdp", None),
            P("fsdp", None),
            P("expert", "fsdp", None),
            P("expert", "fsdp", None),
            P("expert", None, "fsdp"),
            P("expert", None, "fsdp"),
        ),
        out_specs=(
            P("expert", "fsdp"),
            P(("fsdp", "expert"), None),
            P(("fsdp", "expert"), None),
            P("expert", "fsdp", None),
            P("expert", "fsdp", None),
            P("expert", None, "fsdp"),
            P("expert", None, "fsdp"),
        ),
        check_vma=False,
    )
```

profile of v0, /device:TPU:6, one launch (start us, length us, event | category | flops | bytes accessed | tf_op | source)
XLA Modules:
  0.0 1270.2 jit_solution(8579598128162390123)
XLA Ops:
  13.2 18.0 %reduce-window.6 = s32[64,8,128]{2,1,0:T(8,128)S(1)} reduce-window(s32[64,8,128]{2,1,0:T(8,128)S(1)} %fusion.17, s32[]{:T(128)} %constant.30.clone.1), window={size=1x1x128 pad=0_0x0_0x127_0}, to_apply=%region_0.0 | reduce-window | flops 8323072 | bytes 524292 | tf_op jit(solution)/shard_map/reduce-window
  31.9 4.3 scatter_custom_fusion
  36.5 6.2 gather_fusion
  42.7 13.6 %reduce-scatter.11.cloned.1.call-done = f32[128,96]{0,1:T(8,128)} async-done(((f32[128,768]{0,1:T(8,128)}), f32[128,96]{0,1:T(8,128)}) %reduce-scatter.11.cloned.1.call-update) | async-done | bytes 49168 | tf_op jit(solution)/shard_map/reduce_scatter | solution.py:51
  57.3 41.8 %reduce-scatter.9.cloned.1.call-done = f32[128,96]{0,1:T(8,128)} async-done(((f32[128,768]{0,1:T(8,128)}), f32[128,96]{0,1:T(8,128)}) %reduce-scatter.9.cloned.1.call-update) | async-done | bytes 49168 | tf_op jit(solution)/shard_map/reduce_scatter | solution.py:52
  100.0 6.2 gather_fusion.1
  106.2 6.2 gather_fusion.3
  113.5 46.3 %all_to_all.35 = bf16[64,32,96]{2,1,0:T(8,128)(2,1)S(1)} all-to-all(bf16[64,32,96]{2,1,0:T(8,128)(2,1)S(1)} %get-tuple-element.39), channel_id=1, replica_groups=mesh['expert'=64,'fsdp'=8] {'expert'}, dimensions={0} | all-to-all | bytes 786432 | tf_op jit(solution)/shard_map/all_to_all | solution.py:57
  159.8 33.3 %all_to_all.36 = bf16[64,32,96]{2,1,0:T(8,128)(2,1)} all-to-all(bf16[64,32,96]{2,1,0:T(8,128)(2,1)S(1)} %get-tuple-element.40), channel_id=1, replica_groups=mesh['expert'=64,'fsdp'=8] {'expert'}, dimensions={0} | all-to-all | bytes 786432 | tf_op jit(solution)/shard_map/all_to_all | solution.py:60
  193.1 10.6 all-to-all-start
  203.7 7.5 gather_fusion.2
  212.8 24.4 %all-to-all-done = bf16[64,32,96]{2,1,0:T(8,128)(2,1)} async-done(((bf16[64,32,96]{2,1,0:T(8,128)(2,1)}), bf16[64,32,96]{2,1,0:T(8,128)(2,1)}, u32[]{:S(2)}, u32[]{:S(2)}) %all-to-all-start) | async-done | bytes 393248 | tf_op jit(solution)/shard_map/all_to_all | solution.py:63
  237.2 10.9 all-to-all-start.2
  258.3 2.5 copy.68
  260.7 54.4 %all-to-all-done.2 = bf16[64,32,512]{2,1,0:T(8,128)(2,1)S(1)} async-done(((bf16[64,32,512]{2,1,0:T(8,128)(2,1)}), bf16[64,32,512]{2,1,0:T(8,128)(2,1)S(1)}, u32[]{:S(2)}, u32[]{:S(2)}) %all-to-all-start.2) | async-done | bytes 2097184 | tf_op jit(solution)/shard_map/all_to_all | solution.py:56
  315.2 2.6 fusion.19
  319.4 66.9 %all-reduce.4 = (bf16[2048,128]{1,0:T(8,128)(2,1)S(1)}, bf16[2048,128]{1,0:T(8,128)(2,1)}) all-reduce(f32[2048,128]{1,0:T(8,128)} %fusion.19, f32[2048,128]{1,0:T(8,128)} %fusion.22), channel_id=1, replica_groups=mesh['expert'=64,'fsdp'=8] {'fsdp'}, use_global_device_ids=true, to_apply=%region_7.8 | all-reduce | flops 524288 | bytes 3145728 | tf_op jit(solution)/shard_map/psum | solution.py:67
  386.4 2.8 multiply_convert_fusion
  390.6 9.4 all-to-all-start.5
  406.7 23.2 %all-to-all-done.5 = bf16[64,32,96]{2,1,0:T(8,128)(2,1)S(1)} async-done(((bf16[64,32,96]{2,1,0:T(8,128)(2,1)}), bf16[64,32,96]{2,1,0:T(8,128)(2,1)S(1)}, u32[]{:S(2)}, u32[]{:S(2)}) %all-to-all-start.5) | async-done | bytes 393248 | tf_op jit(solution)/shard_map/all_to_all | solution.py:103
  429.9 8.9 all-to-all-start.6
  438.8 77.2 %all-reduce.5 = (bf16[2048,128]{1,0:T(8,128)(2,1)}, bf16[2048,128]{1,0:T(8,128)(2,1)}) all-reduce(f32[2048,128]{1,0:T(8,128)} %fusion.24, f32[2048,128]{1,0:T(8,128)} %fusion.27), channel_id=1, replica_groups=mesh['expert'=64,'fsdp'=8] {'fsdp'}, use_global_device_ids=true, to_apply=%region_8.9 | all-reduce | flops 524288 | bytes 3145728 | tf_op jit(solution)/shard_map/psum | solution.py:90
  519.9 13.4 %all-to-all-start.4 = ((bf16[64,32,512]{2,1,0:T(8,128)(2,1)}), bf16[64,32,512]{2,1,0:T(8,128)(2,1)}, u32[]{:S(2)}, u32[]{:S(2)}) async-start(bf16[64,32,512]{2,1,0:T(8,128)(2,1)} %bitcast.120), calls=%async_computation.6 | async-start | bytes 4194304 | tf_op jit(solution)/shard_map/all_to_all | solution.py:102
  533.4 5.2 gather_fusion.6
  541.8 86.8 %all_gather.7 = bf16[128,768]{0,1:T(8,128)(2,1)S(1)} all-gather(bf16[128,96]{0,1:T(8,128)(2,1)} %copy.73), channel_id=1, replica_groups=mesh['expert'=64,'fsdp'=8] {'fsdp'}, dimensions={1}, use_global_device_ids=true | all-gather | bytes 221184 | tf_op jit(solution)/shard_map/all_gather | solution.py:115
  630.7 3.0 copy.78
  633.9 4.3 gather_fusion.5
  639.4 14.3 %all_gather.6 = bf16[128,768]{0,1:T(8,128)(2,1)S(1)} all-gather(bf16[128,96]{0,1:T(8,128)(2,1)S(1)} %copy.71), channel_id=1, replica_groups=mesh['expert'=64,'fsdp'=8] {'fsdp'}, dimensions={1}, use_global_device_ids=true | all-gather | bytes 221184 | tf_op jit(solution)/shard_map/all_gather | solution.py:114
  655.3 3.1 copy.76
  665.4 5.9 gather_fusion.4
  673.5 274.0 %reduce-scatter.15.cloned.1.call-done = f32[8,768]{1,0:T(8,128)} async-done(((f32[512,768]{1,0:T(8,128)}), f32[8,768]{1,0:T(8,128)}) %reduce-scatter.15.cloned.1.call-update) | async-done | bytes 24592
  947.5 316.2 %reduce-scatter.13.cloned.1.call-done = f32[8,768]{1,0:T(8,128)} async-done(((f32[512,768]{1,0:T(8,128)}), f32[8,768]{1,0:T(8,128)}) %reduce-scatter.13.cloned.1.call-update) | async-done | bytes 24592
  (109 shorter events, 52.7 us)
Async XLA Ops:
  7.2 1.1 copy-start
  7.2 3.3 copy-start.4
  7.2 5.5 copy-start.19
  7.2 49.1 %reduce-scatter.11.cloned.1.call-start = ((), (), s32[]{:S(2)}) async-start(), calls=%async_computation.12 | async-start | bytes 442368 | tf_op jit(solution)/shard_map/reduce_scatter | solution.py:51
  10.4 25.9 %copy-start.17 = (bf16[128,8,96]{0,2,1:T(8,128)(2,1)S(1)}, bf16[128,8,96]{0,2,1:T(8,128)(2,1)}, u32[]{:S(2)}) copy-start(bf16[128,8,96]{0,2,1:T(8,128)(2,1)} %param.11) | copy-start | bytes 589828
  10.4 88.6 %reduce-scatter.9.cloned.1.call-start = ((), (), s32[]{:S(2)}) async-start(), calls=%async_computation.11 | async-start | bytes 442368 | tf_op jit(solution)/shard_map/reduce_scatter | solution.py:52
  31.9 4.7 copy-start.20
  113.5 90.2 %copy-start.1 = (bf16[128,512]{1,0:T(8,128)(2,1)S(1)}, bf16[128,512]{1,0:T(8,128)(2,1)}, u32[]{:S(2)}) copy-start(bf16[128,512]{1,0:T(8,128)(2,1)} %param.9) | copy-start | bytes 393220
  193.1 44.1 %all-to-all-start = ((bf16[64,32,96]{2,1,0:T(8,128)(2,1)}), bf16[64,32,96]{2,1,0:T(8,128)(2,1)}, u32[]{:S(2)}, u32[]{:S(2)}) async-start(bf16[64,32,96]{2,1,0:T(8,128)(2,1)} %get-tuple-element.41), calls=%async_computation | async-start | bytes 1048576 | tf_op jit(solution)/shard_map/all_to_all | solution.py:63
  237.2 78.0 %all-to-all-start.2 = ((bf16[64,32,512]{2,1,0:T(8,128)(2,1)}), bf16[64,32,512]{2,1,0:T(8,128)(2,1)S(1)}, u32[]{:S(2)}, u32[]{:S(2)}) async-start(bf16[64,32,512]{2,1,0:T(8,128)(2,1)} %broadcast_select_fusion), calls=%async_computation.3 | async-start | bytes 4194304 | tf_op jit(solution)/shard_map/all_to_all | solution.py:56
  260.7 57.0 %copy-start.13 = (bf16[1,512,128]{2,1,0:T(8,128)(2,1)S(1)}, bf16[1,512,128]{2,1,0:T(8,128)(2,1)}, u32[]{:S(2)}) copy-start(bf16[1,512,128]{2,1,0:T(8,128)(2,1)} %param.15) | copy-start | bytes 393220
  386.3 2.8 copy-start.15
  386.3 2.8 copy-start.11
  386.4 2.8 copy-start.12
  386.4 2.8 copy-start.16
  386.4 2.8 copy-start.18
  389.6 1.0 copy-start.3
  390.6 39.3 %all-to-all-start.5 = ((bf16[64,32,96]{2,1,0:T(8,128)(2,1)}), bf16[64,32,96]{2,1,0:T(8,128)(2,1)S(1)}, u32[]{:S(2)}, u32[]{:S(2)}) async-start(bf16[64,32,96]{2,1,0:T(8,128)(2,1)} %bitcast.122), calls=%async_computation.7 | async-start | bytes 1048576 | tf_op jit(solution)/shard_map/all_to_all | solution.py:103
  429.9 90.0 %all-to-all-start.6 = ((bf16[64,32,96]{2,1,0:T(8,128)(2,1)}), bf16[64,32,96]{2,1,0:T(8,128)(2,1)}, u32[]{:S(2)}, u32[]{:S(2)}) async-start(bf16[64,32,96]{2,1,0:T(8,128)(2,1)} %bitcast.121), calls=%async_computation.8 | async-start | bytes 1048576 | tf_op jit(solution)/shard_map/all_to_all | solution.py:104
  516.0 1.8 copy-start.7
  516.0 1.9 copy-start.14
  519.9 13.5 %copy-start.21 = (s32[1024,1]{0,1:T(1,128)S(1)}, s32[1024,1]{0,1:T(1,128)}, u32[]{:S(2)}) copy-start(s32[1024,1]{0,1:T(1,128)} %copy-done.20) | copy-start | bytes 12292
  519.9 145.5 %all-to-all-start.4 = ((bf16[64,32,512]{2,1,0:T(8,128)(2,1)}), bf16[64,32,512]{2,1,0:T(8,128)(2,1)}, u32[]{:S(2)}, u32[]{:S(2)}) async-start(bf16[64,32,512]{2,1,0:T(8,128)(2,1)} %bitcast.120), calls=%async_computation.6 | async-start | bytes 4194304 | tf_op jit(solution)/shard_map/all_to_all | solution.py:102
  533.3 414.2 %reduce-scatter.15.cloned.1.call-start = ((), (), s32[]{:S(2)}) async-start(), calls=%async_computation.14 | async-start | bytes 1597440
  628.6 0.7 copy-start.9
  633.8 629.9 %reduce-scatter.13.cloned.1.call-start = ((), (), s32[]{:S(2)}) async-start(), calls=%async_computation.13 | async-start | bytes 1597440
  655.3 3.1 copy-start.2
  658.4 4.1 copy-start.6
  660.4 3.6 copy-start.8
  671.3 1.1 copy-start.5
  671.3 1.2 copy-start.10
Sparse Core Ops, SparseCore 0:
  10.8 45.4 reduce-scatter.10
  59.4 39.6 reduce-scatter.8
  633.9 313.5 reduce-scatter.14
  953.6 310.0 reduce-scatter.12
where the time goes:
time: 1270 us
  waiting for transfers between devices  748 us (59%)
  blocking collectives  325 us (26%)
  local copies, waits for them, and re-layouts  67 us (5%)
  starting transfers between devices  53.4 us (4%)
  matrix products  31.7 us (2%)
  other arithmetic  31.4 us (2%)
  between operations  14.2 us (1%)
    unnamed x6, waiting for transfers between devices  590 us
    all_gather x1, blocking collectives, local(): lax.all_gather(up_sum, 'fsdp', axis=1, tiled=True)  86.8 us
    psum x1, blocking collectives, local(): lax.psum((contract_last(d_gate, gate_right[0]), contract_last(d_up, up_ri...  77.2 us
    psum x1, blocking collectives, local(): lax.psum((jnp.dot(x_rows, gate_left[0], preferred_element_type=jnp.float3...  66.9 us
    all_to_all x1, waiting for transfers between devices, local(): lax.all_to_all(send_rows, 'expert', split_axis=0, concat_axis=0, tiled=True)  54.4 us
    all_to_all x1, blocking collectives, local(): lax.all_to_all(to_slots(gate_act, safe_token), 'expert', split_axis=0, co...  46.3 us
    reduce_scatter x1, waiting for transfers between devices, local(): lax.psum_scatter(part_up, 'fsdp', scatter_dimension=1, tiled=True)  41.8 us
    all_to_all x1, blocking collectives, local(): lax.all_to_all(to_slots(up_act, safe_token), 'expert', split_axis=0, conc...  33.3 us
  transfers between devices with their start and end apart: 9, of which 7 were waited for; matrix products, arithmetic and copies ran while one was open for 8% of the time, Pallas kernels for 0%

commit v1 on v0

v1 whole, which is shorter than its diff:
```python
import jax
import jax.numpy as jnp
from jax import lax
from jax.experimental import pallas as pl
from jax.experimental.pallas import tpu as pltpu
from jax.sharding import PartitionSpec as P

BF = jnp.bfloat16
F32 = jnp.float32
MESH = pl.DeviceIdType.MESH
TOK = 128
FEAT = 512
HID = 96
FF = 768
R = 128
CAP = 32
XROWS = 528
WROWS = 1216
SEMS = 288


def dot(a, b, ca=1, cb=0):
    return lax.dot_general(a, b, (((ca,), (cb,)), ((), ())), preferred_element_type=F32)


def iota(shape, dim):
    return lax.broadcasted_iota(jnp.int32, shape, dim)


SCRATCH = dict(
    xb=((4, 4, XROWS, TOK), BF),
    wb=((4, WROWS, R), BF),
    lt=((4, 2 * R, FEAT), BF),
    ap=((4, 2, 2 * HID, TOK), BF),
    ac=((4, 2 * HID, TOK), BF),
    as_=((4, 2 * HID, TOK), BF),
    az=((3, 2 * HID, TOK), BF),
    ab=((4, 4, 2 * HID, TOK), BF),
    ho=((4, 4, HID, TOK), BF),
    hm=((4, 4, HID, TOK), BF),
    hb=((4, 4, HID, TOK), BF),
    pm=((4 * TOK, 4 * TOK), BF),
    pb=((4, 4 * TOK, 4 * TOK), BF),
    xs=((4, FEAT, 4 * TOK), BF),
    lp=((4, 2, 4, R, TOK), BF),
    lc=((4, 4, R, TOK), BF),
    ls=((4, 4, R, TOK), BF),
    lz=((4, 3, R, TOK), BF),
    lo=((4, 2, 4, R, TOK), BF),
    kp=((4, 2, 4, R, TOK), BF),
    kc=((4, 4, R, TOK), BF),
    ks=((4, 4, R, TOK), BF),
    kz=((4, 3, R, TOK), BF),
    ko=((4, 2, 4, R, TOK), BF),
    dg=((4, 2 * HID, 4 * TOK), BF),
    gp=((4, 4, 2 * HID, TOK), BF),
    gr=((4, 2, HID, TOK), BF),
    gf=((4, 2, 2 * HID, TOK), BF),
    gq=((4, 2 * HID, TOK), BF),
    hr=((2, HID, TOK), BF),
    hf=((2, 2 * HID, TOK), BF),
    gs=((2, 4, 2, HID, TOK), BF),
    dp=((4, 4, FEAT, TOK), BF),
    dr=((4, 2, FEAT // 2, TOK), BF),
    df=((4, 2, FEAT, TOK), BF),
    dq=((4, FEAT, TOK), BF),
    er=((2, FEAT // 2, TOK), BF),
    ef=((2, FEAT, TOK), BF),
    wg=((4, WROWS, R), BF),
    wr=((2, WROWS // 2, R), BF),
    wf=((2, WROWS, R), BF),
    bg=((4, 4, 4, 16, FF), BF),
    bxr=((2, 2, 4, 16, FF), BF),
    bxf=((2, 4, 4, 16, FF), BF),
    by=((4, 4, 16, FF), BF),
    byr=((2, 2, 16, FF), BF),
    byf=((2, 4, 16, FF), BF),
    bz=((4, 16, FF), BF),
    bzr=((2, 16, FF // 2), BF),
    bzf=((2, 16, FF), BF),
)


def kernel(*refs):
    (tokens, routes, hidden, gbase, ubase, gleft, uleft, gright, uright) = refs[:9]
    (o_tok, o_gb, o_ub, o_gl, o_ul, o_gr, o_ur) = refs[9:16]
    s = dict(zip(SCRATCH, refs[16 : 16 + len(SCRATCH)]))
    send_sem, recv_sem = refs[16 + len(SCRATCH) :]

    e = lax.axis_index("expert")
    f = lax.axis_index("fsdp")
    x, y, h = e // 16, (e // 4) % 4, e % 4
    l, c = f // 2, f % 2

    def at(dx=0, dy=0, dh=0, dl=0, dc=0):
        return (
            ((x + dx) % 4) * 16 + ((y + dy) % 4) * 4 + (h + dh) % 4,
            ((l + dl) % 4) * 2 + (c + dc) % 2,
        )

    peers = [dict(dx=1), dict(dx=3), dict(dy=1), dict(dy=2), dict(dy=3), dict(dh=1), dict(dh=2), dict(dh=3)]
    peers += [dict(dl=1), dict(dl=2), dict(dl=3), dict(dc=1)]
    barrier = pltpu.get_barrier_semaphore()
    for peer in peers:
        pl.semaphore_signal(barrier, inc=1, device_id=at(**peer), device_id_type=MESH)
    pl.semaphore_wait(barrier, len(peers))

    started = []

    def send(src, dst, **where):
        n = len(started)
        copy = pltpu.make_async_remote_copy(
            src_ref=src,
            dst_ref=dst,
            send_sem=send_sem.at[n],
            recv_sem=recv_sem.at[n],
            device_id=at(**where),
            device_id_type=MESH,
        )
        copy.start()
        started.append(copy)
        return copy

    class Gather:
        def __init__(self, axis, buf, first, second):
            self.axis, self.buf, self.first, self.second = axis, buf, first, second

        def start(self):
            self.right = send(self.buf(0), self.buf(3), **{self.axis: 1})
            self.left = send(self.buf(0), self.buf(1), **{self.axis: 3})

        def mid(self):
            self.right.wait_recv()
            self.far_right = send(self.first(self.buf(3)), self.first(self.buf(2)), **{self.axis: 1})
            self.left.wait_recv()
            self.far_left = send(self.second(self.buf(1)), self.second(self.buf(2)), **{self.axis: 3})

        def finish(self):
            self.far_right.wait_recv()
            self.far_left.wait_recv()

    class Scatter:
        def __init__(self, axis, part, relay, full, first, second):
            self.axis, self.part, self.relay, self.full = axis, part, relay, full
            self.first, self.second = first, second

        def start(self):
            self.a = send(self.first(self.part(2)), self.relay(0), **{self.axis: 1})
            self.b = send(self.second(self.part(2)), self.relay(1), **{self.axis: 3})

        def mid(self):
            self.a.wait_recv()
            piece = self.first(self.part(1))
            piece[...] = (piece[...].astype(F32) + self.relay(0)[...].astype(F32)).astype(BF)
            self.right = send(self.part(1), self.full(0), **{self.axis: 1})
            self.b.wait_recv()
            piece = self.second(self.part(3))
            piece[...] = (piece[...].astype(F32) + self.relay(1)[...].astype(F32)).astype(BF)
            self.left = send(self.part(3), self.full(1), **{self.axis: 3})

        def finish(self):
            self.right.wait_recv()
            self.left.wait_recv()
            return (
                self.part(0)[...].astype(F32)
                + self.full(0)[...].astype(F32)
                + self.full(1)[...].astype(F32)
            )

    class Reduce:
        def __init__(self, parts, core, sums, lands, out):
            self.parts, self.core, self.sums, self.lands, self.out = parts, core, sums, lands, out

        def start(self):
            self.pair = send(self.parts.at[1 - c], self.core, dc=1)

        def mid(self):
            self.pair.wait_recv()
            self.sums[...] = (
                self.parts[c].astype(F32) + self.core[...].astype(F32)
            ).astype(BF)
            self.hops = [
                send(self.sums.at[(l + i) % 4], self.lands.at[i - 1], dl=i) for i in (1, 2, 3)
            ]

        def finish(self):
            total = self.sums[l].astype(F32)
            for i, hop in enumerate(self.hops):
                hop.wait_recv()
                total = total + self.lands[i].astype(F32)
            return total.astype(BF)

        def share(self):
            self.out[c, l] = self.finish()
            self.back = [
                send(self.out.at[c, l], self.out.at[c, l], dl=i) for i in (1, 2, 3)
            ]

        def across(self):
            for hop in self.back:
                hop.wait_recv()
            self.other = send(self.out.at[c], self.out.at[c], dc=1)

        def done(self):
            self.other.wait_recv()

    def rows(lo, hi):
        return lambda ref: ref.at[lo:hi]

    s["xb"][0, 0, 0:FEAT] = tokens[...].T
    routes_t = routes[...].astype(F32).T
    s["xb"][0, 0, FEAT:XROWS] = jnp.concatenate(
        [routes_t, jnp.zeros((8, TOK), F32)], axis=0
    ).astype(BF)
    x_halves = rows(0, 256), rows(256, XROWS)
    xh = Gather("dh", lambda i: s["xb"].at[i, 0], *x_halves)
    xy = [Gather("dy", lambda i, q=q: s["xb"].at[q, i], *x_halves) for q in range(4)]
    xh.start()
    xy[0].start()
    s["wb"][0, 0:512] = gleft[0]
    s["wb"][0, 512:1024] = uleft[0]
    s["wb"][0, 1024:1120] = gright[0].astype(F32).T.astype(BF)
    s["wb"][0, 1120:1216] = uright[0].astype(F32).T.astype(BF)
    w_halves = rows(0, WROWS // 2), rows(WROWS // 2, WROWS)
    wx = Gather("dx", lambda i: s["wb"].at[i], *w_halves)
    wx.start()

    for half, base in enumerate((gbase, ubase)):
        part = dot(tokens[...], base[...]).T.astype(BF)
        for place in range(4):
            for core in range(2):
                lo = (place * 2 + core) * HID
                s["ap"][place, core, half * HID : (half + 1) * HID] = part[lo : lo + HID]

    class ActReduce(Reduce):
        def start(self):
            self.pair = send(s["ap"].at[:, 1 - c], self.core, dc=1)

        def mid(self):
            self.pair.wait_recv()
            self.sums[...] = (s["ap"][:, c].astype(F32) + self.core[...].astype(F32)).astype(BF)
            self.hops = [
                send(self.sums.at[(l + i) % 4], self.lands.at[i - 1], dl=i) for i in (1, 2, 3)
            ]

    act = ActReduce(None, s["ac"], s["as_"], s["az"], None)
    act.start()
    xy[0].mid()
    wx.mid()

    upper = (iota((TOK, TOK), 0) < iota((TOK, TOK), 1)).astype(BF)
    ranks = iota((64, TOK), 0)
    names = (
        ((x + ranks % 4) % 4) * 16 + ((y + (ranks // 4) % 4) % 4) * 4 + (h + ranks // 16) % 4
    ).astype(F32)
    chosen = [(names == routes_t[k : k + 1]).astype(F32) for k in range(8)]
    ranks_f = ranks.astype(F32)
    order = dot(sum(chosen).astype(BF), upper) + ranks_f * CAP
    slot = [jnp.sum(chosen[k] * order, axis=0, keepdims=True) for k in range(8)]
    hid = hidden[...].reshape(8 * TOK, HID)
    hid_t = jnp.transpose(hidden[...].astype(F32), (1, 2, 0)).astype(BF)
    hid_t = jnp.concatenate([hid_t[k] for k in range(8)], axis=1)
    for place in range(16):
        want = (iota((TOK, TOK), 0) + place * TOK).astype(F32)
        pick = jnp.concatenate([(slot[k] == want).astype(BF) for k in range(8)], axis=1)
        s["ho"][place // 4, place % 4] = dot(hid_t, pick, 1, 1).astype(BF)
    s["hb"][0, 0] = s["ho"][0, 0]
    hh = [None] + [send(s["ho"].at[i], s["hm"].at[4 - i], dh=i) for i in (1, 2, 3)]
    hy = {0: [send(s["ho"].at[0, i], s["hb"].at[0, 4 - i], dy=i) for i in (1, 2, 3)]}

    def pass_hidden(i):
        hh[4 - i].wait_recv()
        s["hb"][i, 0] = s["hm"][i, 0]
        hy[i] = [send(s["hm"].at[i, j], s["hb"].at[i, 4 - j], dy=j) for j in (1, 2, 3)]

    act.mid()
    r4, c4 = iota((512, 512), 0), iota((512, 512), 1)
    s["pm"][...] = (
        (r4 // 128 == (c4 // 32) % 4) & ((r4 // 32) % 4 == c4 // 128) & (r4 % 32 == c4 % 32)
    ).astype(BF)
    s["pb"][...] = jnp.zeros_like(s["pb"])

    xh.mid()
    xy[1].start()
    xy[3].start()

    s["ab"][0, 0] = act.finish()
    a_halves = rows(0, HID), rows(HID, 2 * HID)
    ah = Gather("dh", lambda i: s["ab"].at[i, 0], *a_halves)
    ay = [Gather("dy", lambda i, q=q: s["ab"].at[q, i], *a_halves) for q in range(4)]
    ah.start()
    ay[0].start()

    experts = [(((x + j) % 4) * 16 + y * 4 + h).astype(F32) for j in range(4)]
    group_sum = (iota((16, TOK), 1) // 8 == iota((16, TOK), 0)).astype(BF)

    def select(q):
        named = []
        for b in range(4):
            block = s["xb"][q, b, FEAT:XROWS].astype(F32)[0:8]
            named += [(block == experts[j]).astype(F32) for j in range(4)]
        hit = dot(group_sum, jnp.concatenate(named, axis=0).astype(BF))
        place = jnp.where(hit > 0.5, dot(hit.astype(BF), upper), -1.0)
        want = iota((CAP, TOK), 0).astype(F32)
        for b in range(4):
            for j in range(4):
                row = place[b * 4 + j : b * 4 + j + 1]
                s["pb"][q, j * 128 + b * CAP : j * 128 + (b + 1) * CAP, b * TOK : (b + 1) * TOK] = (
                    row == want
                ).astype(BF)
        feats = jnp.concatenate([s["xb"][q, b, 0:FEAT] for b in range(4)], axis=1)
        s["xs"][q] = dot(feats, s["pb"][q], 1, 1).astype(BF)
        for j in range(4):
            low = dot(s["lt"][j], s["xs"][q, :, j * TOK : (j + 1) * TOK]).astype(BF)
            s["lp"][q, 0, j] = low[0:R]
            s["lp"][q, 1, j] = low[R : 2 * R]

    low = [
        Reduce(s["lp"].at[q], s["lc"].at[q], s["ls"].at[q], s["lz"].at[q], s["lo"].at[q])
        for q in range(4)
    ]
    dlow = [
        Reduce(s["kp"].at[q], s["kc"].at[q], s["ks"].at[q], s["kz"].at[q], s["ko"].at[q])
        for q in range(4)
    ]

    wx.finish()
    for j in range(4):
        s["lt"][j, 0:R] = s["wb"][j, 0:512].T
        s["lt"][j, R : 2 * R] = s["wb"][j, 512:1024].T
    xy[0].finish()
    select(0)
    low[0].start()
    xy[1].mid()
    xy[3].mid()
    xh.finish()
    xy[2].start()
    low[0].mid()
    ah.mid()
    ay[1].start()
    ay[3].start()
    ay[0].mid()
    xy[1].finish()
    select(1)
    low[1].start()
    xy[2].mid()
    low[0].share()
    low[1].mid()
    xy[3].finish()
    select(3)
    low[3].start()
    ay[1].mid()
    ay[3].mid()
    ah.finish()
    ay[2].start()
    low[1].share()
    low[0].across()
    low[3].mid()
    xy[2].finish()
    select(2)
    low[2].start()
    ay[2].mid()
    low[3].share()
    low[1].across()
    low[2].mid()
    for i in (1, 3, 2):
        pass_hidden(i)
    low[2].share()
    low[3].across()
    low[2].across()

    def middle(q):
        for j in (1, 2, 3):
            hy[q][j - 1].wait_recv()
        acts = jnp.concatenate([s["ab"][q, b] for b in range(4)], axis=1)
        acts = dot(acts, s["pb"][q], 1, 1)
        cot = jnp.concatenate([s["hb"][q, b] for b in range(4)], axis=1)
        cot = dot(cot, s["pm"][...], 1, 1)
        gate = acts[0:HID] + jnp.concatenate(
            [dot(s["wb"][j, 1024:1120], s["lo"][q, 0, j]) for j in range(4)], axis=1
        )
        up = acts[HID : 2 * HID] + jnp.concatenate(
            [dot(s["wb"][j, 1120:1216], s["lo"][q, 1, j]) for j in range(4)], axis=1
        )
        sigma = jax.nn.sigmoid(gate)
        s["dg"][q, 0:HID] = (cot * up * sigma * (1.0 + gate * (1.0 - sigma))).astype(BF)
        s["dg"][q, HID : 2 * HID] = (cot * gate * sigma).astype(BF)
        for j in range(4):
            for half in range(2):
                s["kp"][q, half, j] = dot(
                    s["wb"][j, 1024 + half * HID : 1120 + half * HID],
                    s["dg"][q, half * HID : (half + 1) * HID, j * TOK : (j + 1) * TOK],
                    0,
                    0,
                ).astype(BF)

    def sums(q):
        part = dot(s["dg"][q], s["pb"][q]).astype(BF)
        for b in range(4):
            s["gp"][q, b] = part[:, b * TOK : (b + 1) * TOK]

    gy = [
        Scatter(
            "dy",
            lambda i, q=q: s["gp"].at[q, i],
            lambda i, q=q: s["gr"].at[q, i],
            lambda i, q=q: s["gf"].at[q, i],
            *a_halves,
        )
        for q in range(4)
    ]
    gh = Scatter(
        "dh", lambda i: s["gq"].at[i], lambda i: s["hr"].at[i], lambda i: s["hf"].at[i], *a_halves
    )
    d_halves = rows(0, 256), rows(256, 512)
    dy = [
        Scatter(
            "dy",
            lambda i, q=q: s["dp"].at[q, i],
            lambda i, q=q: s["dr"].at[q, i],
            lambda i, q=q: s["df"].at[q, i],
            *d_halves,
        )
        for q in range(4)
    ]
    dh = Scatter(
        "dh", lambda i: s["dq"].at[i], lambda i: s["er"].at[i], lambda i: s["ef"].at[i], *d_halves
    )

    def inputs(q):
        part = None
        for j in range(4):
            left = jnp.concatenate([s["wb"][j, 0:512], s["wb"][j, 512:1024]], axis=1)
            back = jnp.concatenate([s["ko"][q, 0, j], s["ko"][q, 1, j]], axis=0)
            s["dp"][q, j] = dot(left, back).astype(BF)
        delta = jnp.concatenate([s["dp"][q, j] for j in range(4)], axis=1)
        part = dot(delta, s["pb"][q]).astype(BF)
        for b in range(4):
            s["dp"][q, b] = part[:, b * TOK : (b + 1) * TOK]

    xy_left = [ay[0], ay[1], ay[3], ay[2]]
    back_order = (2, 1, 3, 0)
    low_done = set()
    for q in (0, 1, 3, 2):
        low[q].done()
    for a in xy_left:
        a.finish()
    for n, q in enumerate(back_order):
        middle(q)
        dlow[q].start()
        sums(q)
        gy[q].start()
        if n >= 1:
            p = back_order[n - 1]
            dlow[p].mid()
            gy[p].mid()
        if n >= 2:
            p = back_order[n - 2]
            dlow[p].share()
            s["gq"][p] = gy[p].finish().astype(BF)
            if p == 2:
                gh.start()
    dlow[0].mid()
    gy[0].mid()
    dlow[2].across()
    dlow[3].share()
    s["gq"][3] = gy[3].finish().astype(BF)
    gh.mid()
    dlow[1].across()
    dlow[0].share()
    s["gq"][0] = gy[0].finish().astype(BF)
    dlow[2].done()
    inputs(2)
    dy[2].start()
    dlow[3].across()
    dlow[1].done()
    inputs(1)
    dy[1].start()
    dy[2].mid()
    dlow[0].across()
    total = gh.finish().astype(BF)
    s["gs"][0, l, c] = total[0:HID]
    s["gs"][1, l, c] = total[HID : 2 * HID]
    gs_back = [
        send(s["gs"].at[:, l, c], s["gs"].at[:, l, c], dl=i) for i in (1, 2, 3)
    ]
    dlow[3].done()
    inputs(3)
    dy[3].start()
    dy[1].mid()
    s["dq"][2] = dy[2].finish().astype(BF)
    dh.start()
    for hop in gs_back:
        hop.wait_recv()
    gs_core = send(s["gs"].at[:, :, c], s["gs"].at[:, :, c], dc=1)
    dlow[0].done()
    inputs(0)
    dy[0].start()
    dy[3].mid()
    s["dq"][1] = dy[1].finish().astype(BF)
    s["dq"][3] = dy[3].finish().astype(BF)
    dh.mid()
    dy[0].mid()

    gs_core.wait_recv()
    whole = [s["gs"][half].reshape(FF, TOK) for half in range(2)]
    feats_t = s["xb"][0, 0, 0:FEAT]
    for place in range(4):
        piece = feats_t[place * 128 : (place + 1) * 128]
        both = jnp.concatenate(
            [dot(piece, whole[half], 1, 1).reshape(16, 8, FF) for half in range(2)], axis=1
        )
        s["bg"][place] = both.astype(BF).reshape(4, 4, 16, FF)

    bx = Scatter(
        "dx",
        lambda i: s["bg"].at[(x + i) % 4],
        lambda i: s["bxr"].at[i],
        lambda i: s["bxf"].at[i],
        rows(0, 2),
        rows(2, 4),
    )
    bx.start()

    for j in range(4):
        slots = jnp.concatenate(
            [s["xs"][q, :, j * TOK : (j + 1) * TOK] for q in range(4)], axis=1
        )
        for half in range(2):
            back = jnp.concatenate([s["ko"][q, half, j] for q in range(4)], axis=1)
            s["wg"][j, half * 512 : (half + 1) * 512] = dot(slots, back, 1, 1).astype(BF)
            lows = jnp.concatenate([s["lo"][q, half, j] for q in range(4)], axis=1)
            dgs = jnp.concatenate(
                [
                    s["dg"][q, half * HID : (half + 1) * HID, j * TOK : (j + 1) * TOK]
                    for q in range(4)
                ],
                axis=1,
            )
            s["wg"][j, 1024 + half * HID : 1120 + half * HID] = dot(dgs, lows, 1, 1).astype(BF)
    wgx = Scatter(
        "dx", lambda i: s["wg"].at[i], lambda i: s["wr"].at[i], lambda i: s["wf"].at[i], *w_halves
    )
    wgx.start()
    bx.mid()
    s["dq"][0] = dy[0].finish().astype(BF)
    wgx.mid()
    base_part = dot(gbase[...], whole[0]) + dot(ubase[...], whole[1])
    s["by"][...] = bx.finish().astype(BF)
    by = Scatter(
        "dy",
        lambda i: s["by"].at[(y + i) % 4],
        lambda i: s["byr"].at[i],
        lambda i: s["byf"].at[i],
        rows(0, 2),
        rows(2, 4),
    )
    by.start()
    o_tok[...] = (dh.finish() + base_part).T.astype(BF)
    by.mid()
    s["bz"][...] = by.finish().astype(BF)
    bz = Scatter(
        "dh",
        lambda i: s["bz"].at[(h + i) % 4],
        lambda i: s["bzr"].at[i],
        lambda i: s["bzf"].at[i],
        lambda ref: ref.at[:, 0 : FF // 2],
        lambda ref: ref.at[:, FF // 2 : FF],
    )
    bz.start()
    grads = wgx.finish()
    o_gl[0] = grads[0:512]
    o_ul[0] = grads[512:1024]
    o_gr[0] = grads[1024:1120].T
    o_ur[0] = grads[1120:1216].T
    bz.mid()
    grad = bz.finish()
    o_gb[...] = grad[0:8]
    o_ub[...] = grad[8:16]
    for copy in started:
        copy.wait_send()


def local(*args):
    vmem = pl.BlockSpec(memory_space=pltpu.VMEM)
    shapes = [
        ((TOK, FEAT), BF),
        ((8, FF), F32),
        ((8, FF), F32),
        ((1, FEAT, R), F32),
        ((1, FEAT, R), F32),
        ((1, R, HID), F32),
        ((1, R, HID), F32),
    ]
    return pl.pallas_call(
        kernel,
        out_shape=[jax.ShapeDtypeStruct(*shape) for shape in shapes],
        in_specs=[vmem] * 9,
        out_specs=[vmem] * 7,
        scratch_shapes=[pltpu.VMEM(*shape) for shape in SCRATCH.values()]
        + [pltpu.SemaphoreType.DMA((SEMS,)), pltpu.SemaphoreType.DMA((SEMS,))],
        compiler_params=pltpu.CompilerParams(
            collective_id=0, has_side_effects=True, vmem_limit_bytes=56 * 1024 * 1024
        ),
    )(*args)


def solution(mesh):
    return jax.shard_map(
        local,
        mesh=mesh,
        in_specs=(
            P("expert", "fsdp"),
            P("expert", None),
            P("expert", None, "fsdp"),
            P("fsdp", None),
            P("fsdp", None),
            P("expert", "fsdp", None),
            P("expert", "fsdp", None),
            P("expert", None, "fsdp"),
            P("expert", None, "fsdp"),
        ),
        out_specs=(
            P("expert", "fsdp"),
            P(("fsdp", "expert"), None),
            P(("fsdp", "expert"), None),
            P("expert", "fsdp", None),
            P("expert", "fsdp", None),
            P("expert", None, "fsdp"),
            P("expert", None, "fsdp"),
        ),
        check_vma=False,
    )
```

time: 1270 us -> 201 us (0.16)
  the two profiles are of different devices: /device:TPU:6 before, /device:TPU:96 now
where the time goes in v1:
time: 201 us; the launch traced here: 200 us
  Pallas kernels  188 us (94%)
  local copies, waits for them, and re-layouts  11.7 us (6%)
    pallas_call x1, Pallas kernels, local(): pl.pallas_call(kernel, out_shape=[jax.ShapeDtypeStruct(*shape) for shape...  188 us
    unnamed x23, local copies, waits for them, and re-layouts  8.56 us

profile of v1, /device:TPU:96, one launch (start us, length us, event | category | flops | bytes accessed | tf_op | source)
XLA Modules:
  0.0 200.3 jit_solution(5184167140437267768)
XLA Ops:
  0.6 0.0 copy-start.3
  0.6 1.5 copy.18.refs_7_
  2.1 0.0 copy-done.3
  2.1 0.0 copy-start.6
  2.1 0.7 copy.19.refs_8_
  2.8 0.0 copy-done.6
  2.8 0.7 copy.16.refs_1_
  3.6 1.8 copy.17.refs_2_
  5.4 187.9 %shard_map.144 = (bf16[128,512]{1,0:T(8,128)(2,1)}, f32[8,768]{1,0:T(8,128)}, f32[8,768]{1,0:T(8,128)}, f32[1,512,128]{2,1,0:T(8,128)}, f32[1,512,128]{2,1,0:T(8...) custom-call(bf16[128,512]{1,0:T(8,128)(2,1)} %refs_0_.1, s32[128,8]{1,0:T(8,128)} %copy.16.refs_1_, ...), custom_call_target="tpu_custom_call" | custom-call | tf_op jit(solution)/shard_map/pallas_call | solution.py:595
  193.2 0.0 copy-start.2
  193.3 1.6 copy.20
  194.8 0.0 copy-start.1
  194.8 1.6 copy.21
  196.4 0.0 copy-done.2
  196.4 0.0 copy-start.5
  196.4 0.7 copy.27
  197.1 0.1 copy-done.5
  197.2 0.0 copy-start.4
  197.2 0.6 copy.28
  197.8 0.1 copy-done.4
  197.9 0.6 copy.29
  198.5 0.0 copy-done.1
  198.5 0.0 copy-start
  198.5 0.7 copy.30
  199.2 0.3 copy-done
  199.6 0.7 copy.31
Async XLA Ops:
  0.6 1.5 copy-start.3
  2.1 0.7 copy-start.6
  193.2 3.2 %copy-start.2 = (bf16[128,512]{1,0:T(8,128)(2,1)S(1)}, bf16[128,512]{1,0:T(8,128)(2,1)}, u32[]{:S(2)}) copy-start(bf16[128,512]{1,0:T(8,128)(2,1)} %get-tuple-element.21) | copy-start | bytes 393220
  194.8 3.7 %copy-start.1 = (f32[1,512,128]{2,1,0:T(8,128)S(1)}, f32[1,512,128]{2,1,0:T(8,128)}, u32[]{:S(2)}) copy-start(f32[1,512,128]{2,1,0:T(8,128)} %get-tuple-element.24) | copy-start | bytes 786436
  196.4 0.7 copy-start.5
  197.2 0.7 copy-start.4
  198.5 1.0 copy-start

commit v2 on v0

v2 whole, which is shorter than its diff:
```python
import types

import jax
import jax.numpy as jnp
from jax import lax
from jax.experimental import pallas as pl
from jax.experimental.pallas import tpu as pltpu
from jax.sharding import PartitionSpec as P

BF = jnp.bfloat16
F32 = jnp.float32
MESH = pl.DeviceIdType.MESH
TOK = 128
FEAT = 512
HID = 96
FF = 768
R = 128
CAP = 32
XROWS = 528
WROWS = 1216
SEMS = 288


def dot(a, b, ca=1, cb=0):
    return lax.dot_general(a, b, (((ca,), (cb,)), ((), ())), preferred_element_type=F32)


def iota(shape, dim):
    return lax.broadcasted_iota(jnp.int32, shape, dim)


SCRATCH = dict(
    hi=((8, HID, TOK), BF),
    gi=((FEAT, FF), BF),
    ui=((FEAT, FF), BF),
    xb=((4, 4, XROWS, TOK), BF),
    wb=((4, WROWS, R), BF),
    lt=((4, 2 * R, FEAT), BF),
    ap=((2, 4, 2 * HID, TOK), F32),
    ac=((4, 2 * HID, TOK), F32),
    as_=((4, 2 * HID, TOK), BF),
    az=((3, 2 * HID, TOK), BF),
    ab=((4, 4, 2 * HID, TOK), BF),
    ho=((4, 4, HID, TOK), BF),
    hw=((2, 2, HID, TOK), BF),
    hm=((4, 4, HID, TOK), BF),
    hb=((4, 4, HID, TOK), BF),
    pm=((4 * TOK, 4 * TOK), BF),
    pb=((4, 4 * TOK, 4 * TOK), BF),
    xs=((4, FEAT, 4 * TOK), BF),
    lp=((4, 2, 4, R, TOK), F32),
    lc=((4, 4, R, TOK), F32),
    ls=((4, 4, R, TOK), BF),
    lz=((4, 2, 4, R, TOK), BF),
    lo=((4, 2, 4, R, TOK), BF),
    kp=((4, 2, 4, R, TOK), F32),
    kc=((4, 4, R, TOK), F32),
    ks=((4, 4, R, TOK), BF),
    kz=((4, 2, 4, R, TOK), BF),
    ko=((4, 2, 4, R, TOK), BF),
    dg=((4, 2 * HID, 4 * TOK), BF),
    gp=((4, 4, 2 * HID, TOK), BF),
    gw=((4, 4, 2 * HID, TOK), F32),
    gf=((4, 3, 2 * HID, TOK), BF),
    gq=((4, 2 * HID, TOK), BF),
    gv=((4, 2 * HID, TOK), F32),
    hr=((2, HID, TOK), BF),
    hf=((2, 2 * HID, TOK), BF),
    gs=((2, 4, 2, HID, TOK), BF),
    dp=((2, 4, 4, FEAT // 2, TOK), BF),
    dw=((2, 4, 4, FEAT // 2, TOK), F32),
    dr=((2, 4, 2, FEAT // 4, TOK), BF),
    df=((2, 4, 2, FEAT // 2, TOK), BF),
    dq=((2, 4, FEAT // 2, TOK), BF),
    dv=((2, 4, FEAT // 2, TOK), F32),
    er=((2, 2, FEAT // 4, TOK), BF),
    ef=((2, 2, FEAT // 2, TOK), BF),
    wg=((4, WROWS, R), BF),
    ww=((4, WROWS, R), F32),
    wr=((2, WROWS // 2, R), BF),
    wf=((2, WROWS, R), BF),
    bg=((2, 4, 4, 4, 16, FF // 2), BF),
    bw=((2, 4, 4, 4, 16, FF // 2), F32),
    bxr=((2, 2, 2, 4, 16, FF // 2), BF),
    bxf=((2, 2, 4, 4, 16, FF // 2), BF),
    by=((2, 4, 4, 16, FF // 2), BF),
    byw=((2, 4, 4, 16, FF // 2), F32),
    byf=((2, 3, 4, 16, FF // 2), BF),
    bz=((2, 4, 16, FF // 2), BF),
    bzw=((2, 4, 16, FF // 2), F32),
    bzf=((2, 3, 16, FF // 2), BF),
)


ORDER = (
    0, 3, 15, 20, 21, 22, 16, 17, 1, 9, 4, 18, 19, 40, 23, 24, 27, 6, 5, 48, 49, 50, 51, 2, 12, 39, 41, 10, 28, 11,
    7, 52, 44, 100, 101, 102, 13, 103, 25, 33, 14, 126, 8, 74, 34, 127, 30, 128, 129, 47, 53, 104, 35, 42, 75, 76,
    54, 77, 45, 130, 105, 43, 29, 55, 56, 57, 31, 26, 36, 63, 131, 58, 78, 64, 106, 107, 37, 108, 109, 115, 46, 110,
    38, 116, 132, 79, 59, 133, 134, 135, 141, 142, 136, 111, 80, 32, 60, 81, 82, 83, 89, 90, 137, 84, 112, 143, 152,
    61, 62, 70, 71, 138, 85, 91, 117, 153, 113, 65, 114, 66, 67, 122, 118, 119, 123, 86, 139, 140, 144, 148, 145,
    149, 120, 154, 155, 124, 150, 87, 88, 173, 92, 93, 96, 97, 174, 156, 151, 183, 146, 98, 157, 158, 68, 165, 166,
    147, 178, 99, 125, 184, 159, 94, 95, 121, 167, 175, 179, 160, 161, 162, 163, 168, 169, 170, 171, 72, 164, 73,
    182, 185, 186, 176, 69, 180, 177, 181, 172,
)


class Plan:
    def __init__(self):
        self.steps = {}

    def add(self, name, run, after=(), cost=0.1, link=None, size=0.0):
        assert name not in self.steps
        self.steps[name] = (run, tuple(after), cost, link, size)

    def order(self):
        names, done = list(self.steps), set()
        assert sorted(ORDER) == list(range(len(names)))
        for place in ORDER:
            assert all(dep.lstrip(">") in done for dep in self.steps[names[place]][1])
            done.add(names[place])
        return [names[place] for place in ORDER]


def kernel(*refs):
    (tokens, routes, hidden_in, gbase_in, ubase_in, gleft, uleft, gright, uright) = refs[:9]
    (o_tok, o_gb, o_ub, o_gl, o_ul, o_gr, o_ur) = refs[9:16]
    s = types.SimpleNamespace(**dict(zip(SCRATCH, refs[16 : 16 + len(SCRATCH)])))
    send_sem, recv_sem, read_sem = refs[16 + len(SCRATCH) :]
    hidden, gbase, ubase = s.hi, s.gi, s.ui

    e = lax.axis_index("expert")
    f = lax.axis_index("fsdp")
    x, y, h = e // 16, (e // 4) % 4, e % 4
    l, c = f // 2, f % 2

    def at(dx=0, dy=0, dh=0, dl=0, dc=0):
        return (
            ((x + dx) % 4) * 16 + ((y + dy) % 4) * 4 + (h + dh) % 4,
            ((l + dl) % 4) * 2 + (c + dc) % 2,
        )

    peers = [dict(dx=1), dict(dx=3), dict(dy=1), dict(dy=2), dict(dy=3), dict(dh=1), dict(dh=2), dict(dh=3)]
    peers += [dict(dl=1), dict(dl=2), dict(dl=3), dict(dc=1)]
    barrier = pltpu.get_barrier_semaphore()
    for peer in peers:
        pl.semaphore_signal(barrier, inc=1, device_id=at(**peer), device_id_type=MESH)

    reads = [
        pltpu.make_async_copy(src, dst, read_sem.at[n])
        for n, (src, dst) in enumerate(
            [
                (gleft.at[0], s.wb.at[0, 0:512]),
                (uleft.at[0], s.wb.at[0, 512:1024]),
                (gright.at[0], s.wb.at[0, 1024:1120]),
                (uright.at[0], s.wb.at[0, 1120:1216]),
                (gbase_in, gbase),
                (ubase_in, ubase),
                (hidden_in, hidden),
            ]
        )
    ]
    for read in reads:
        read.start()

    started = []

    class Copy:
        def __init__(self, src, dst, here, there, where):
            self.src, self.dst, self.here, self.there, self.where = src, dst, here, there, where
            self.n = len(started)
            started.append(self)
            self.run(here, lambda copy: copy.start())

        def run(self, when, act):
            def go():
                act(
                    pltpu.make_async_remote_copy(
                        src_ref=self.src,
                        dst_ref=self.dst,
                        send_sem=send_sem.at[self.n],
                        recv_sem=recv_sem.at[self.n],
                        device_id=at(**self.where),
                        device_id_type=MESH,
                    )
                )

            if when is None:
                go()
            else:
                pl.when(when)(go)

        def wait_recv(self):
            self.run(self.there, lambda copy: copy.wait_recv())

        def wait_send(self):
            self.run(self.here, lambda copy: copy.wait_send())

    def send(src, dst, here=None, there=None, **where):
        return Copy(src, dst, here, there, where)

    edge, inner = (l == 0) | (l == 3), (l == 1) | (l == 2)

    class Gather:
        def __init__(self, axis, buf, first, second):
            self.axis, self.buf, self.first, self.second = axis, buf, first, second

        def start(self):
            self.right = send(self.buf(0), self.buf(3), **{self.axis: 1})
            self.left = send(self.buf(0), self.buf(1), **{self.axis: 3})

        def mid(self):
            self.right.wait_recv()
            self.far_right = send(self.first(self.buf(3)), self.first(self.buf(2)), **{self.axis: 1})
            self.left.wait_recv()
            self.far_left = send(self.second(self.buf(1)), self.second(self.buf(2)), **{self.axis: 3})

        def finish(self):
            self.far_right.wait_recv()
            self.far_left.wait_recv()

    class Scatter:
        def __init__(self, axis, part, wide, relay, full, first, second):
            self.axis, self.part, self.wide, self.relay, self.full = axis, part, wide, relay, full
            self.first, self.second = first, second

        def start(self):
            self.a = send(self.first(self.part(2)), self.relay(0), **{self.axis: 1})
            self.b = send(self.second(self.part(2)), self.relay(1), **{self.axis: 3})

        def mid(self):
            for copy, half, i in ((self.a, self.first, 1), (self.b, self.second, 3)):
                copy.wait_recv()
                lane = self.relay(i // 2)[...].astype(F32)
                half(self.part(i))[...] = (half(self.wide(i))[...] + lane).astype(BF)
            self.right = send(self.part(1), self.full(0), **{self.axis: 1})
            self.left = send(self.part(3), self.full(1), **{self.axis: 3})

        def finish(self):
            self.right.wait_recv()
            self.left.wait_recv()
            return (
                self.wide(0)[...]
                + self.full(0)[...].astype(F32)
                + self.full(1)[...].astype(F32)
            )

    class Direct:
        def __init__(self, axis, part, wide, full):
            self.axis, self.part, self.wide, self.full = axis, part, wide, full

        def start(self):
            self.copies = [
                send(self.part(i), self.full(i - 1), **{self.axis: i}) for i in (1, 3, 2)
            ]

        def finish(self):
            total = self.wide(0)[...]
            for i, copy in zip((1, 3, 2), self.copies):
                copy.wait_recv()
                total = total + self.full(i - 1)[...].astype(F32)
            return total

    class Reduce:
        def __init__(self, parts, core, sums, lands):
            self.parts, self.core, self.sums, self.lands = parts, core, sums, lands

        def start(self):
            self.pair = send(self.parts.at[1 - c], self.core, dc=1)

        def mid(self):
            self.pair.wait_recv()
            total = self.parts[c] + self.core[...]
            self.parts[c] = total
            self.sums[...] = total.astype(BF)
            self.hops = [
                send(self.sums.at[(l + i) % 4], self.lands.at[i - 1], dl=i) for i in (1, 2, 3)
            ]

        def finish(self):
            total = self.parts[c, l]
            for i, hop in enumerate(self.hops):
                hop.wait_recv()
                total = total + self.lands[i].astype(F32)
            return total.astype(BF)

    class AllReduce:
        def __init__(self, parts, core, sums, lands, out):
            self.parts, self.core, self.sums, self.lands, self.out = parts, core, sums, lands, out

        def start(self):
            self.pair = send(self.parts.at[1 - c], self.core, dc=1)

        def outer(self):
            self.pair.wait_recv()
            total = self.parts[c] + self.core[...]
            self.parts[c] = total

            @pl.when(edge)
            def _():
                self.sums[...] = total.astype(BF)

            self.up = send(self.sums, self.lands.at[0], edge, inner, dl=1 - 2 * (l % 2))

        def swap(self):
            self.up.wait_recv()

            @pl.when(inner)
            def _():
                total = self.parts[c] + self.lands[0].astype(F32)
                self.parts[c] = total
                self.sums[...] = total.astype(BF)

            self.over = send(self.sums, self.lands.at[1], inner, inner, dl=3 - 2 * l)

        def share(self):
            self.over.wait_recv()

            @pl.when(inner)
            def _():
                self.out[c] = (self.parts[c] + self.lands[1].astype(F32)).astype(BF)

            self.down = send(self.out.at[c], self.out.at[c], inner, edge, dl=1 - 2 * (l % 2))
            self.inner_pair = send(self.out.at[c], self.out.at[c], inner, inner, dc=1)

        def across(self):
            self.down.wait_recv()
            self.edge_pair = send(self.out.at[c], self.out.at[c], edge, edge, dc=1)

        def done(self):
            self.inner_pair.wait_recv()
            self.edge_pair.wait_recv()

    def rows(lo, hi):
        return lambda ref: ref.at[lo:hi]

    routes_t = routes[...].astype(F32)
    s.xb[0, 0, 0:FEAT] = tokens[...].T
    s.xb[0, 0, FEAT:XROWS] = jnp.concatenate(
        [routes_t, jnp.zeros((8, TOK), F32)], axis=0
    ).astype(BF)
    pl.semaphore_wait(barrier, len(peers))

    plan = Plan()

    upper = (iota((TOK, TOK), 0) < iota((TOK, TOK), 1)).astype(BF)

    def own_weights():
        for read in reads[0:4]:
            read.wait()

    def own_partials():
        reads[4].wait()
        reads[5].wait()
        for half, base in enumerate((gbase, ubase)):
            part = dot(tokens[...], base[...]).T
            for place in range(4):
                for core in range(2):
                    lo = (place * 2 + core) * HID
                    s.ap[core, place, half * HID : (half + 1) * HID] = part[lo : lo + HID]

    def own_slots():
        reads[6].wait()
        ranks = iota((64, TOK), 0)
        names = (
            ((x + ranks % 4) % 4) * 16 + ((y + (ranks // 4) % 4) % 4) * 4 + (h + ranks // 16) % 4
        ).astype(F32)
        chosen = [(names == routes_t[k : k + 1]).astype(F32) for k in range(8)]
        order = dot(sum(chosen).astype(BF), upper) + ranks.astype(F32) * CAP
        slot = [jnp.sum(chosen[k] * order, axis=0, keepdims=True) for k in range(8)]
        hid_t = jnp.concatenate([hidden[k] for k in range(8)], axis=1)
        for place in range(16):
            want = (iota((TOK, TOK), 0) + place * TOK).astype(F32)
            pick = jnp.concatenate([(slot[k] == want).astype(BF) for k in range(8)], axis=1)
            s.ho[place // 4, place % 4] = dot(hid_t, pick, 1, 1).astype(BF)
        s.hb[0, 0] = s.ho[0, 0]

    def tables():
        r4, c4 = iota((512, 512), 0), iota((512, 512), 1)
        s.pm[...] = (
            (r4 // 128 == (c4 // 32) % 4) & ((r4 // 32) % 4 == c4 // 128) & (r4 % 32 == c4 % 32)
        ).astype(BF)
        s.pb[...] = jnp.zeros_like(s.pb)

    def gather(name, task, link, size, after=()):
        plan.add(name + "0", task.start, after, 0.1, link, size)
        plan.add(name + "1", task.mid, [">" + name + "0"], 0.1, link, size / 2)
        plan.add(name + "2", task.finish, [">" + name + "1"], 0.05)

    def scatter(name, task, link, size, after, last, cost=0.3):
        plan.add(name + "0", task.start, after, 0.1, link, size / 2)
        plan.add(name + "1", task.mid, [">" + name + "0"] + list(after), cost, link, size)
        plan.add(name + "2", last, [">" + name + "1"], cost)

    def direct(name, task, link, size, after, last, cost=0.2):
        plan.add(name + "0", task.start, after, 0.1, link, size)
        plan.add(name + "2", last, [">" + name + "0"], cost)

    x_halves = rows(0, 256), rows(256, XROWS)
    gather("xh", Gather("dh", lambda i: s.xb.at[i, 0], *x_halves), "z", 1.0)
    for q in (0, 1, 3, 2):
        task = Gather("dy", lambda i, q=q: s.xb.at[q, i], *x_halves)
        gather(f"xy{q}", task, "y", 0.25, [[], ["xh1"], ["xh2"], ["xh1"]][q])
    plan.add("wts", own_weights, [], 0.2)
    w_halves = rows(0, WROWS // 2), rows(WROWS // 2, WROWS)
    gather("wx", Gather("dx", lambda i: s.wb.at[i], *w_halves), "x", 0.6, ["wts"])

    def turn():
        for j in range(4):
            s.lt[j, 0:R] = s.wb[j, 0:512].T
            s.lt[j, R : 2 * R] = s.wb[j, 512:1024].T

    plan.add("lt", turn, ["wx2"], 0.5)

    act = Reduce(s.ap, s.ac, s.as_, s.az)

    def own_act():
        s.ab[0, 0] = act.finish()

    plan.add("actp", own_partials, [], 0.8)
    plan.add("act0", act.start, ["actp"], 0.1, "core", 0.375)
    plan.add("act1", act.mid, [">act0"], 0.3, "z", 0.375)
    plan.add("act2", own_act, [">act1"], 0.2)
    a_halves = rows(0, HID), rows(HID, 2 * HID)
    gather("ah", Gather("dh", lambda i: s.ab.at[i, 0], *a_halves), "z", 0.375, ["act2"])
    for q in (0, 1, 3, 2):
        task = Gather("dy", lambda i, q=q: s.ab.at[q, i], *a_halves)
        gather(f"ay{q}", task, "y", 0.1, [["act2"], ["ah1"], ["ah2"], ["ah1"]][q])

    hop = {}

    def hidden_near():
        hop["near"] = [send(s.ho.at[i], s.hm.at[4 - i], dh=i) for i in (1, 3)]

    def hidden_far():
        hop["far"] = [
            send(s.ho.at[2, 0:2], s.hw.at[0], dh=1),
            send(s.ho.at[2, 2:4], s.hw.at[1], dh=3),
        ]

    def hidden_on():
        hop["on"] = []
        for n, copy in enumerate(hop["far"]):
            copy.wait_recv()
            hop["on"].append(
                send(s.hw.at[n], s.hm.at[2, 2 * n : 2 * n + 2], dh=(1, 3)[n])
            )

    def hidden_pass(q):
        if q in (1, 3):
            hop["near"][{3: 0, 1: 1}[q]].wait_recv()
        elif q == 2:
            for copy in hop["on"]:
                copy.wait_recv()
        held = s.ho if q == 0 else s.hm
        if q:
            s.hb[q, 0] = s.hm[q, 0]
        hop[q] = [send(held.at[q, j], s.hb.at[q, 4 - j], dy=j) for j in (1, 2, 3)]

    plan.add("slots", own_slots, [], 1.5)
    plan.add("tab", tables, [], 0.4)
    plan.add("hn", hidden_near, ["slots", "xh1"], 0.1, "z", 0.75)
    plan.add("hf", hidden_far, ["slots", "xh1"], 0.1, "z", 0.375)
    plan.add("ho", hidden_on, [">hf"], 0.1, "z", 0.375)
    for q in range(4):
        from_ = [["slots"], [">hn"], [">ho"], [">hn"]][q]
        plan.add(f"hy{q}", lambda q=q: hidden_pass(q), from_, 0.1, "y", 0.15)

    experts = [(((x + j) % 4) * 16 + y * 4 + h).astype(F32) for j in range(4)]
    group_sum = (iota((16, TOK), 1) // 8 == iota((16, TOK), 0)).astype(BF)

    def select(q):
        named = []
        for b in range(4):
            block = s.xb[q, b, FEAT:XROWS].astype(F32)[0:8]
            named += [(block == experts[j]).astype(F32) for j in range(4)]
        hit = dot(group_sum, jnp.concatenate(named, axis=0).astype(BF))
        place = jnp.where(hit > 0.5, dot(hit.astype(BF), upper), -1.0)
        want = iota((CAP, TOK), 0).astype(F32)
        for b in range(4):
            for j in range(4):
                row = place[b * 4 + j : b * 4 + j + 1]
                s.pb[q, j * 128 + b * CAP : j * 128 + (b + 1) * CAP, b * TOK : (b + 1) * TOK] = (
                    row == want
                ).astype(BF)
        feats = jnp.concatenate([s.xb[q, b, 0:FEAT] for b in range(4)], axis=1)
        s.xs[q] = dot(feats, s.pb[q], 1, 1).astype(BF)

    def project(q):
        for j in range(4):
            value = dot(s.lt[j], s.xs[q, :, j * TOK : (j + 1) * TOK])
            s.lp[q, 0, j] = value[0:R]
            s.lp[q, 1, j] = value[R : 2 * R]

    def allreduce(name, task, after):
        plan.add(name + "0", task.start, after, 0.1, "core", 0.25)
        plan.add(name + "1", task.outer, [">" + name + "0"], 0.2, "zi", 0.25)
        plan.add(name + "2", task.swap, [">" + name + "1"], 0.2, "zm", 0.25)
        plan.add(name + "3", task.share, [">" + name + "2"], 0.2, "zo", 0.25)
        plan.add(name + "4", task.across, [">" + name + "3"], 0.1, "core", 0.125)
        plan.add(name + "5", task.done, [">" + name + "4"], 0.05)

    low = [
        AllReduce(s.lp.at[q], s.lc.at[q], s.ls.at[q], s.lz.at[q], s.lo.at[q])
        for q in range(4)
    ]
    dlow = [
        AllReduce(s.kp.at[q], s.kc.at[q], s.ks.at[q], s.kz.at[q], s.ko.at[q])
        for q in range(4)
    ]

    def middle(q):
        for copy in hop[q]:
            copy.wait_recv()
        acts = jnp.concatenate([s.ab[q, b] for b in range(4)], axis=1)
        acts = dot(acts, s.pb[q], 1, 1)
        cot = jnp.concatenate([s.hb[q, b] for b in range(4)], axis=1)
        cot = dot(cot, s.pm[...], 1, 1)
        gate = acts[0:HID] + jnp.concatenate(
            [dot(s.wb[j, 1024:1120], s.lo[q, 0, j]) for j in range(4)], axis=1
        )
        up = acts[HID : 2 * HID] + jnp.concatenate(
            [dot(s.wb[j, 1120:1216], s.lo[q, 1, j]) for j in range(4)], axis=1
        )
        sigma = jax.nn.sigmoid(gate)
        s.dg[q, 0:HID] = (cot * up * sigma * (1.0 + gate * (1.0 - sigma))).astype(BF)
        s.dg[q, HID : 2 * HID] = (cot * gate * sigma).astype(BF)
        for j in range(4):
            for half in range(2):
                s.kp[q, half, j] = dot(
                    s.wb[j, 1024 + half * HID : 1120 + half * HID],
                    s.dg[q, half * HID : (half + 1) * HID, j * TOK : (j + 1) * TOK],
                    0,
                    0,
                )

    def sums(q):
        part = dot(s.dg[q], s.pb[q])
        for b in range(4):
            s.gw[q, b] = part[:, b * TOK : (b + 1) * TOK]
            s.gp[q, b] = part[:, b * TOK : (b + 1) * TOK].astype(BF)

    def inputs(q, n):
        delta = []
        for j in range(4):
            lo = n * (FEAT // 2)
            left = jnp.concatenate(
                [s.wb[j, lo : lo + 256], s.wb[j, 512 + lo : 768 + lo]], axis=1
            )
            back = jnp.concatenate([s.ko[q, 0, j], s.ko[q, 1, j]], axis=0)
            delta.append(dot(left, back).astype(BF))
        part = dot(jnp.concatenate(delta, axis=1), s.pb[q])
        for b in range(4):
            s.dw[n, q, b] = part[:, b * TOK : (b + 1) * TOK]
            s.dp[n, q, b] = part[:, b * TOK : (b + 1) * TOK].astype(BF)

    def keep(task, wide, narrow):
        total = task.finish()
        wide[...] = total
        narrow[...] = total.astype(BF)

    d_halves = rows(0, 128), rows(128, 256)
    for q in (0, 1, 3, 2):
        plan.add(f"sel{q}", lambda q=q: select(q), ["tab", f"xy{q}2"], 0.5)
        plan.add(f"prj{q}", lambda q=q: project(q), ["lt", f"sel{q}"], 0.3)
        allreduce(f"lo{q}", low[q], [f"prj{q}"])
        plan.add(f"mid{q}", lambda q=q: middle(q), [f"lo{q}5", f"ay{q}2", f">hy{q}"], 0.5)
        allreduce(f"dl{q}", dlow[q], [f"mid{q}"])
        plan.add(f"sum{q}", lambda q=q: sums(q), [f"mid{q}"], 0.2)
        task = Direct(
            "dy",
            lambda i, q=q: s.gp.at[q, i],
            lambda i, q=q: s.gw.at[q, i],
            lambda i, q=q: s.gf.at[q, i],
        )
        direct(
            f"gy{q}", task, "y", 0.24, [f"sum{q}"],
            lambda q=q, task=task: keep(task, s.gv.at[q], s.gq.at[q]), 0.15,
        )
        for n in range(2):
            plan.add(f"inp{q}{n}", lambda q=q, n=n: inputs(q, n), [f"dl{q}5"], 0.25)
            task = Scatter(
                "dy",
                lambda i, q=q, n=n: s.dp.at[n, q, i],
                lambda i, q=q, n=n: s.dw.at[n, q, i],
                lambda i, q=q, n=n: s.dr.at[n, q, i],
                lambda i, q=q, n=n: s.df.at[n, q, i],
                *d_halves,
            )
            scatter(
                f"d{n}y{q}", task, "y", 0.125, [f"inp{q}{n}"],
                lambda q=q, n=n, task=task: keep(task, s.dv.at[n, q], s.dq.at[n, q]), 0.15,
            )

    kept = {}

    def ring_h(name, task, size, last, cost):
        along = name[:-1] + "y"
        near = [along + f"{q}2" for q in (1, 3)]
        plan.add(name + "0", task.start, [along + "22"], 0.1, "z", size / 2)
        plan.add(name + "1", task.mid, [">" + name + "0"] + near, cost, "z", size)
        plan.add(name + "2", last, [">" + name + "1", along + "02"], cost)

    gh = Scatter(
        "dh",
        lambda i: s.gq.at[i],
        lambda i: s.gv.at[i],
        lambda i: s.hr.at[i],
        lambda i: s.hf.at[i],
        *a_halves,
    )

    def token_sums():
        total = gh.finish().astype(BF)
        s.gs[0, l, c] = total[0:HID]
        s.gs[1, l, c] = total[HID : 2 * HID]
        kept["gs"] = [
            send(s.gs.at[:, l, c], s.gs.at[:, l, c], dl=i) for i in (1, 2, 3)
        ]

    def token_sums_across():
        for copy in kept["gs"]:
            copy.wait_recv()
        kept["gc"] = send(s.gs.at[:, :, c], s.gs.at[:, :, c], dc=1)

    ring_h("gh", gh, 0.375, lambda: None, 0.1)
    plan.add("gs0", token_sums, ["gh2"], 0.2, "z", 0.375)
    plan.add("gs1", token_sums_across, [">gs0"], 0.1, "core", 0.2)

    def base_grads(n):
        if n == 0:
            kept["gc"].wait_recv()
        lo = n * (FF // 2)
        whole = [s.gs[half].reshape(FF, TOK)[lo : lo + FF // 2] for half in range(2)]
        for place in range(4):
            piece = s.xb[0, 0, place * 128 : (place + 1) * 128]
            both = jnp.concatenate(
                [dot(piece, whole[half], 1, 1).reshape(16, 8, FF // 2) for half in range(2)],
                axis=1,
            ).reshape(4, 4, 16, FF // 2)
            s.bw[n, place] = both
            s.bg[n, place] = both.astype(BF)

    def base_out(n, task):
        grad = task.finish()
        lo = n * (FF // 2)
        o_gb[:, lo : lo + FF // 2] = grad[0:8]
        o_ub[:, lo : lo + FF // 2] = grad[8:16]

    for n in range(2):
        plan.add(f"bas{n}", lambda n=n: base_grads(n), [">gs1"] + ["bas0"] * n, 0.35)
        bx = Scatter(
            "dx",
            lambda i, n=n: s.bg.at[n, (x + i) % 4],
            lambda i, n=n: s.bw.at[n, (x + i) % 4],
            lambda i, n=n: s.bxr.at[n, i],
            lambda i, n=n: s.bxf.at[n, i],
            rows(0, 2),
            rows(2, 4),
        )
        by = Direct(
            "dy",
            lambda i, n=n: s.by.at[n, (y + i) % 4],
            lambda i, n=n: s.byw.at[n, (y + i) % 4],
            lambda i, n=n: s.byf.at[n, i],
        )
        bz = Direct(
            "dh",
            lambda i, n=n: s.bz.at[n, (h + i) % 4],
            lambda i, n=n: s.bzw.at[n, (h + i) % 4],
            lambda i, n=n: s.bzf.at[n, i],
        )
        scatter(
            f"bx{n}", bx, "x", 0.375, [f"bas{n}"],
            lambda n=n, bx=bx: keep(bx, s.byw.at[n], s.by.at[n]), 0.2,
        )
        direct(
            f"by{n}", by, "y", 0.14, [f"bx{n}2"],
            lambda n=n, by=by: keep(by, s.bzw.at[n], s.bz.at[n]), 0.1,
        )
        direct(f"bz{n}", bz, "z", 0.25, [f"by{n}2"], lambda n=n, bz=bz: base_out(n, bz), 0.1)

    def weight_grads():
        for j in range(4):
            slots = jnp.concatenate(
                [s.xs[q, :, j * TOK : (j + 1) * TOK] for q in range(4)], axis=1
            )
            for half in range(2):
                back = jnp.concatenate([s.ko[q, half, j] for q in range(4)], axis=1)
                left = dot(slots, back, 1, 1)
                s.ww[j, half * 512 : (half + 1) * 512] = left
                s.wg[j, half * 512 : (half + 1) * 512] = left.astype(BF)
                lows = jnp.concatenate([s.lo[q, half, j] for q in range(4)], axis=1)
                dgs = jnp.concatenate(
                    [
                        s.dg[q, half * HID : (half + 1) * HID, j * TOK : (j + 1) * TOK]
                        for q in range(4)
                    ],
                    axis=1,
                )
                right = dot(dgs, lows, 1, 1)
                s.ww[j, 1024 + half * HID : 1120 + half * HID] = right
                s.wg[j, 1024 + half * HID : 1120 + half * HID] = right.astype(BF)

    wgx = Scatter(
        "dx",
        lambda i: s.wg.at[i],
        lambda i: s.ww.at[i],
        lambda i: s.wr.at[i],
        lambda i: s.wf.at[i],
        *w_halves,
    )

    def weight_out():
        grads = wgx.finish()
        o_gl[0] = grads[0:512]
        o_ul[0] = grads[512:1024]
        o_gr[0] = grads[1024:1120]
        o_ur[0] = grads[1120:1216]

    plan.add("wgr", weight_grads, [f"dl{q}5" for q in range(4)], 0.8)
    scatter("wgx", wgx, "x", 0.6, ["wgr"], weight_out, 0.3)

    dh = [
        Scatter(
            "dh",
            lambda i, n=n: s.dq.at[n, i],
            lambda i, n=n: s.dv.at[n, i],
            lambda i, n=n: s.er.at[n, i],
            lambda i, n=n: s.ef.at[n, i],
            *d_halves,
        )
        for n in range(2)
    ]

    def base_input(n):
        whole = [s.gs[half].reshape(FF, TOK) for half in range(2)]
        lo = n * (FEAT // 2)
        part = dot(gbase[lo : lo + 256], whole[0]) + dot(ubase[lo : lo + 256], whole[1])
        s.dv[n, 0] = s.dv[n, 0] + part

    def token_out(n):
        lo = n * (FEAT // 2)
        o_tok[:, lo : lo + 256] = dh[n].finish().T.astype(BF)

    for n in range(2):
        plan.add(f"bin{n}", lambda n=n: base_input(n), [">gs1", "bas0", f"d{n}y02"], 0.3)
        ring_h(f"d{n}h", dh[n], 0.5, lambda: None, 0.2)
        plan.add(f"tok{n}", lambda n=n: token_out(n), [f"d{n}h2", f"bin{n}"], 0.2)

    for name in plan.order():
        plan.steps[name][0]()
    for copy in started:
        copy.wait_send()


def hand_on(*refs):
    for given, taken in zip(refs[:7], refs[7:]):
        taken[...] = given[...]


def local(tokens, routes, hidden, gbase, ubase, gleft, uleft, gright, uright):
    vmem = pl.BlockSpec(memory_space=pltpu.VMEM)
    anywhere = pl.BlockSpec(memory_space=pl.ANY)
    shapes = [
        ((TOK, FEAT), BF),
        ((8, FF), F32),
        ((8, FF), F32),
        ((1, FEAT, R), F32),
        ((1, FEAT, R), F32),
        ((1, HID, R), F32),
        ((1, HID, R), F32),
    ]
    outs = pl.pallas_call(
        kernel,
        out_shape=[jax.ShapeDtypeStruct(*shape) for shape in shapes],
        in_specs=[vmem] * 2 + [anywhere] * 7,
        out_specs=[vmem] * 7,
        scratch_shapes=[pltpu.VMEM(*shape) for shape in SCRATCH.values()]
        + [pltpu.SemaphoreType.DMA((SEMS,)), pltpu.SemaphoreType.DMA((SEMS,)), pltpu.SemaphoreType.DMA((7,))],
        compiler_params=pltpu.CompilerParams(
            collective_id=0, has_side_effects=True, vmem_limit_bytes=60 * 1024 * 1024
        ),
    )(
        tokens,
        routes.T,
        jnp.transpose(hidden, (1, 2, 0)),
        gbase,
        ubase,
        gleft,
        uleft,
        jnp.swapaxes(gright, 1, 2),
        jnp.swapaxes(uright, 1, 2),
    )
    outs = pl.pallas_call(
        hand_on,
        out_shape=[jax.ShapeDtypeStruct(*shape) for shape in shapes],
        in_specs=[vmem] * 7,
        out_specs=[vmem] * 7,
    )(*outs)
    return (*outs[:5], jnp.swapaxes(outs[5], 1, 2), jnp.swapaxes(outs[6], 1, 2))


def solution(mesh):
    return jax.shard_map(
        local,
        mesh=mesh,
        in_specs=(
            P("expert", "fsdp"),
            P("expert", None),
            P("expert", None, "fsdp"),
            P("fsdp", None),
            P("fsdp", None),
            P("expert", "fsdp", None),
            P("expert", "fsdp", None),
            P("expert", None, "fsdp"),
            P("expert", None, "fsdp"),
        ),
        out_specs=(
            P("expert", "fsdp"),
            P(("fsdp", "expert"), None),
            P(("fsdp", "expert"), None),
            P("expert", "fsdp", None),
            P("expert", "fsdp", None),
            P("expert", None, "fsdp"),
            P("expert", None, "fsdp"),
        ),
        check_vma=False,
    )
```

time: 1270 us -> 155 us (0.12)
  waiting for transfers between devices: 748 us -> 0 us
  blocking collectives: 325 us -> 0 us
  Pallas kernels: 0 us -> 153 us
  local copies, waits for them, and re-layouts: 67 us -> 0 us
  starting transfers between devices: 53.4 us -> 0 us
  matrix products: 31.7 us -> 0 us
  other arithmetic: 31.4 us -> 0 us
  between operations: 14.2 us -> 0.64 us
    unnamed x6 -> x0, waiting for transfers between devices: 590 us -> none
    pallas_call x0 -> x2, Pallas kernels: none -> 153 us  [the longest x1 151 us: local(): pl.pallas_call(kernel, out_shape=[jax.ShapeDtypeStruct(*shape) for shape...]
    psum x2 -> x0, blocking collectives: 144 us -> none  [the longest x1 77.2 us: local(): lax.psum((contract_last(d_gate, gate_right[0]), contract_last(d_up, up_ri...]
    all_to_all x5 -> x0, waiting for transfers between devices: 102 us -> none  [the longest x1 54.4 us: local(): lax.all_to_all(send_rows, 'expert', split_axis=0, concat_axis=0, tiled=True)]
    all_gather x2 -> x0, blocking collectives: 101 us -> none  [the longest x1 86.8 us: local(): lax.all_gather(up_sum, 'fsdp', axis=1, tiled=True)]
    all_to_all x2 -> x0, blocking collectives: 79.6 us -> none  [the longest x1 46.3 us: local(): lax.all_to_all(to_slots(gate_act, safe_token), 'expert', split_axis=0, co...]
    reduce_scatter x2 -> x0, waiting for transfers between devices: 55.4 us -> none  [the longest x1 41.8 us: local(): lax.psum_scatter(part_up, 'fsdp', scatter_dimension=1, tiled=True)]
    all_to_all x5 -> x0, starting transfers between devices: 53.2 us -> none  [the longest x1 13.4 us: local(): lax.all_to_all(delta_send, 'expert', split_axis=0, concat_axis=0, tiled=T...]
  transfers between devices with their start and end apart: 9 -> 0, of which waited for: 7 -> 0; matrix products, arithmetic and copies ran while one was open for 8% -> 0% of each run, Pallas kernels for 0% -> 0%
where the time goes in v2:
time: 155 us; the launch traced here: 154 us
  Pallas kernels  153 us (99%)
    pallas_call x1, Pallas kernels, local(): pl.pallas_call(kernel, out_shape=[jax.ShapeDtypeStruct(*shape) for shape...  151 us

profile of v2, /device:TPU:6, one launch (start us, length us, event | category | flops | bytes accessed | tf_op | source)
XLA Modules:
  0.0 154.0 jit_solution(16012083223327058258)
XLA Ops:
  0.6 151.4 %shard_map.144 = (bf16[128,512]{1,0:T(8,128)(2,1)}, f32[8,768]{1,0:T(8,128)}, f32[8,768]{1,0:T(8,128)}, f32[1,512,128]{2,1,0:T(8,128)}, f32[1,512,128]{2,1,0:T(8...) custom-call(bf16[128,512]{1,0:T(8,128)(2,1)} %refs_0_.1, s32[8,128]{1,0:T(8,128)} %bitcast.9, ...), custom_call_target="tpu_custom_call" | custom-call | tf_op jit(solution)/shard_map/pallas_call | solution.py:773
  152.0 2.0 %shard_map.145 = (bf16[128,512]{1,0:T(8,128)(2,1)}, f32[8,768]{1,0:T(8,128)}, f32[8,768]{1,0:T(8,128)}, f32[1,512,128]{2,1,0:T(8,128)}, f32[1,512,128]{2,1,0:T(8...) custom-call(bf16[128,512]{1,0:T(8,128)(2,1)} %get-tuple-element.21.refs_0_, f32[8,768]{1,0:T(8,128)} %get-tuple-element.22.refs_1_, ...), custom_call_target="tpu_custom_call" | custom-call | tf_op jit(solution)/shard_map/pallas_call | solution.py:794

commit v3 on v2

--- a/solution.py
+++ b/solution.py
@@ -30,6 +30,8 @@
 
 
 SCRATCH = dict(
+    ti=((TOK, FEAT), BF),
+    ri=((8, TOK), jnp.int32),
     hi=((8, HID, TOK), BF),
     gi=((FEAT, FF), BF),
     ui=((FEAT, FF), BF),
@@ -62,11 +64,7 @@
     gp=((4, 4, 2 * HID, TOK), BF),
     gw=((4, 4, 2 * HID, TOK), F32),
     gf=((4, 3, 2 * HID, TOK), BF),
-    gq=((4, 2 * HID, TOK), BF),
-    gv=((4, 2 * HID, TOK), F32),
-    hr=((2, HID, TOK), BF),
-    hf=((2, 2 * HID, TOK), BF),
-    gs=((2, 4, 2, HID, TOK), BF),
+    gs=((4, 2, 4, 2 * HID, TOK), BF),
     dp=((2, 4, 4, FEAT // 2, TOK), BF),
     dw=((2, 4, 4, FEAT // 2, TOK), F32),
     dr=((2, 4, 2, FEAT // 4, TOK), BF),
@@ -88,19 +86,20 @@
     byf=((2, 3, 4, 16, FF // 2), BF),
     bz=((2, 4, 16, FF // 2), BF),
     bzw=((2, 4, 16, FF // 2), F32),
-    bzf=((2, 3, 16, FF // 2), BF),
+    bzr=((2, 2, 16, FF // 2), BF),
+    bzf=((2, 2, 16, FF // 2), BF),
 )
 
 
 ORDER = (
-    0, 3, 15, 20, 21, 22, 16, 17, 1, 9, 4, 18, 19, 40, 23, 24, 27, 6, 5, 48, 49, 50, 51, 2, 12, 39, 41, 10, 28, 11,
-    7, 52, 44, 100, 101, 102, 13, 103, 25, 33, 14, 126, 8, 74, 34, 127, 30, 128, 129, 47, 53, 104, 35, 42, 75, 76,
-    54, 77, 45, 130, 105, 43, 29, 55, 56, 57, 31, 26, 36, 63, 131, 58, 78, 64, 106, 107, 37, 108, 109, 115, 46, 110,
-    38, 116, 132, 79, 59, 133, 134, 135, 141, 142, 136, 111, 80, 32, 60, 81, 82, 83, 89, 90, 137, 84, 112, 143, 152,
-    61, 62, 70, 71, 138, 85, 91, 117, 153, 113, 65, 114, 66, 67, 122, 118, 119, 123, 86, 139, 140, 144, 148, 145,
-    149, 120, 154, 155, 124, 150, 87, 88, 173, 92, 93, 96, 97, 174, 156, 151, 183, 146, 98, 157, 158, 68, 165, 166,
-    147, 178, 99, 125, 184, 159, 94, 95, 121, 167, 175, 179, 160, 161, 162, 163, 168, 169, 170, 171, 72, 164, 73,
-    182, 185, 186, 176, 69, 180, 177, 181, 172,
+    0, 20, 15, 16, 21, 22, 3, 4, 40, 17, 5, 48, 1, 9, 18, 19, 49, 50, 6, 51, 23, 24, 10, 11, 108, 109, 110, 2, 12,
+    111, 52, 39, 44, 13, 27, 41, 25, 53, 33, 14, 138, 139, 140, 30, 141, 112, 31, 7, 8, 42, 45, 78, 79, 80, 47, 81,
+    28, 26, 54, 36, 142, 113, 34, 55, 29, 56, 57, 63, 64, 43, 114, 82, 65, 58, 143, 37, 35, 115, 116, 123, 124, 117,
+    118, 46, 66, 144, 83, 59, 32, 125, 38, 145, 146, 147, 153, 154, 67, 119, 148, 84, 60, 85, 126, 86, 87, 93, 94,
+    155, 120, 149, 88, 61, 127, 95, 156, 121, 150, 89, 62, 74, 122, 130, 134, 131, 157, 75, 96, 151, 135, 90, 128,
+    70, 71, 152, 160, 161, 164, 165, 68, 158, 97, 136, 162, 91, 166, 92, 100, 101, 129, 137, 159, 132, 69, 98, 163,
+    190, 104, 105, 167, 194, 102, 99, 168, 169, 177, 178, 133, 103, 106, 191, 186, 170, 187, 179, 107, 195, 171,
+    172, 180, 181, 76, 188, 173, 174, 72, 182, 183, 175, 184, 77, 196, 197, 73, 192, 193, 176, 189, 185,
 )
 
 
@@ -122,11 +121,11 @@
 
 
 def kernel(*refs):
-    (tokens, routes, hidden_in, gbase_in, ubase_in, gleft, uleft, gright, uright) = refs[:9]
+    (tokens_in, routes_in, hidden_in, gbase_in, ubase_in, gleft, uleft, gright, uright) = refs[:9]
     (o_tok, o_gb, o_ub, o_gl, o_ul, o_gr, o_ur) = refs[9:16]
     s = types.SimpleNamespace(**dict(zip(SCRATCH, refs[16 : 16 + len(SCRATCH)])))
     send_sem, recv_sem, read_sem = refs[16 + len(SCRATCH) :]
-    hidden, gbase, ubase = s.hi, s.gi, s.ui
+    tokens, routes, hidden, gbase, ubase = s.ti, s.ri, s.hi, s.gi, s.ui
 
     e = lax.axis_index("expert")
     f = lax.axis_index("fsdp")
@@ -139,7 +138,7 @@
             ((l + dl) % 4) * 2 + (c + dc) % 2,
         )
 
-    peers = [dict(dx=1), dict(dx=3), dict(dy=1), dict(dy=2), dict(dy=3), dict(dh=1), dict(dh=2), dict(dh=3)]
+    peers = [dict(dx=1), dict(dx=3), dict(dy=1), dict(dy=2), dict(dy=3), dict(dh=1), dict(dh=3)]
     peers += [dict(dl=1), dict(dl=2), dict(dl=3), dict(dc=1)]
     barrier = pltpu.get_barrier_semaphore()
     for peer in peers:
@@ -156,10 +155,12 @@
                 (gbase_in, gbase),
                 (ubase_in, ubase),
                 (hidden_in, hidden),
+                (tokens_in, tokens),
+                (routes_in, routes),
             ]
         )
     ]
-    for read in reads:
+    for read in reads[::-1]:
         read.start()
 
     started = []
@@ -330,9 +331,39 @@
             self.inner_pair.wait_recv()
             self.edge_pair.wait_recv()
 
+    class Share:
+        def __init__(self, out, task):
+            self.out, self.task = out, task
+
+        def start(self):
+            self.out[c, l] = self.task.finish().astype(BF)
+            own = self.out.at[c, l]
+            self.up = send(own, own, edge, inner, dl=1 - 2 * (l % 2))
+
+        def swap(self):
+            self.up.wait_recv()
+            pair = self.out.at[c, pl.ds(2 * (l // 2), 2)]
+            self.over = send(pair, pair, inner, inner, dl=3 - 2 * l)
+
+        def back(self):
+            self.over.wait_recv()
+            others = self.out.at[c, pl.ds(jnp.maximum(2 - l, 0) % 2, 3)]
+            self.down = send(others, others, inner, edge, dl=1 - 2 * (l % 2))
+            self.inner_pair = send(self.out.at[c], self.out.at[c], inner, inner, dc=1)
+
+        def across(self):
+            self.down.wait_recv()
+            self.edge_pair = send(self.out.at[c], self.out.at[c], edge, edge, dc=1)
+
+        def done(self):
+            self.inner_pair.wait_recv()
+            self.edge_pair.wait_recv()
+
     def rows(lo, hi):
         return lambda ref: ref.at[lo:hi]
 
+    reads[7].wait()
+    reads[8].wait()
     routes_t = routes[...].astype(F32)
     s.xb[0, 0, 0:FEAT] = tokens[...].T
     s.xb[0, 0, FEAT:XROWS] = jnp.concatenate(
@@ -386,10 +417,10 @@
         plan.add(name + "1", task.mid, [">" + name + "0"], 0.1, link, size / 2)
         plan.add(name + "2", task.finish, [">" + name + "1"], 0.05)
 
-    def scatter(name, task, link, size, after, last, cost=0.3):
+    def scatter(name, task, link, size, after, last, cost=0.3, late=()):
         plan.add(name + "0", task.start, after, 0.1, link, size / 2)
-        plan.add(name + "1", task.mid, [">" + name + "0"] + list(after), cost, link, size)
-        plan.add(name + "2", last, [">" + name + "1"], cost)
+        plan.add(name + "1", task.mid, [">" + name + "0"] + list(after), 0.15, link, size)
+        plan.add(name + "2", last, [">" + name + "1"] + list(late), cost)
 
     def direct(name, task, link, size, after, last, cost=0.2):
         plan.add(name + "0", task.start, after, 0.1, link, size)
@@ -558,6 +589,21 @@
         wide[...] = total
         narrow[...] = total.astype(BF)
 
+    def token_sums(q, half, first=0, last=4):
+        return [
+            s.gs[q, core, place, half * HID : (half + 1) * HID]
+            for place in range(first, last)
+            for core in range(2)
+        ]
+
+    def keep_inputs(q, n, task):
+        lo = n * (FEAT // 2)
+        total = task.finish()
+        for half, base in enumerate((gbase, ubase)):
+            total = total + dot(base[lo : lo + 256], jnp.concatenate(token_sums(q, half), axis=0))
+        s.dv[n, q] = total
+        s.dq[n, q] = total.astype(BF)
+
     d_halves = rows(0, 128), rows(128, 256)
     for q in (0, 1, 3, 2):
         plan.add(f"sel{q}", lambda q=q: select(q), ["tab", f"xy{q}2"], 0.5)
@@ -572,10 +618,13 @@
             lambda i, q=q: s.gw.at[q, i],
             lambda i, q=q: s.gf.at[q, i],
         )
-        direct(
-            f"gy{q}", task, "y", 0.24, [f"sum{q}"],
-            lambda q=q, task=task: keep(task, s.gv.at[q], s.gq.at[q]), 0.15,
-        )
+        share = Share(s.gs.at[q], task)
+        plan.add(f"gy{q}0", task.start, [f"sum{q}"], 0.1, "y", 0.24)
+        plan.add(f"ga{q}0", share.start, [f">gy{q}0"], 0.15, "zi", 0.095)
+        plan.add(f"ga{q}1", share.swap, [f">ga{q}0"], 0.1, "zm", 0.19)
+        plan.add(f"ga{q}2", share.back, [f">ga{q}1"], 0.1, "zo", 0.28)
+        plan.add(f"ga{q}3", share.across, [f">ga{q}2"], 0.1, "core", 0.19)
+        plan.add(f"ga{q}4", share.done, [f">ga{q}3"], 0.05)
         for n in range(2):
             plan.add(f"inp{q}{n}", lambda q=q, n=n: inputs(q, n), [f"dl{q}5"], 0.25)
             task = Scatter(
@@ -588,10 +637,9 @@
             )
             scatter(
                 f"d{n}y{q}", task, "y", 0.125, [f"inp{q}{n}"],
-                lambda q=q, n=n, task=task: keep(task, s.dv.at[n, q], s.dq.at[n, q]), 0.15,
+                lambda q=q, n=n, task=task: keep_inputs(q, n, task), 0.35, [f"ga{q}4"],
             )
 
-    kept = {}
 
     def ring_h(name, task, size, last, cost):
         along = name[:-1] + "y"
@@ -600,45 +648,31 @@
         plan.add(name + "1", task.mid, [">" + name + "0"] + near, cost, "z", size)
         plan.add(name + "2", last, [">" + name + "1", along + "02"], cost)
 
-    gh = Scatter(
-        "dh",
-        lambda i: s.gq.at[i],
-        lambda i: s.gv.at[i],
-        lambda i: s.hr.at[i],
-        lambda i: s.hf.at[i],
-        *a_halves,
-    )
-
-    def token_sums():
-        total = gh.finish().astype(BF)
-        s.gs[0, l, c] = total[0:HID]
-        s.gs[1, l, c] = total[HID : 2 * HID]
-        kept["gs"] = [
-            send(s.gs.at[:, l, c], s.gs.at[:, l, c], dl=i) for i in (1, 2, 3)
+    def base_grads(n):
+        whole = [
+            jnp.concatenate(
+                [
+                    jnp.concatenate(token_sums(q, half, 2 * n, 2 * n + 2), axis=0)
+                    for q in range(4)
+                ],
+                axis=1,
+            )
+            for half in range(2)
         ]
-
-    def token_sums_across():
-        for copy in kept["gs"]:
-            copy.wait_recv()
-        kept["gc"] = send(s.gs.at[:, :, c], s.gs.at[:, :, c], dc=1)
-
-    ring_h("gh", gh, 0.375, lambda: None, 0.1)
-    plan.add("gs0", token_sums, ["gh2"], 0.2, "z", 0.375)
-    plan.add("gs1", token_sums_across, [">gs0"], 0.1, "core", 0.2)
-
-    def base_grads(n):
-        if n == 0:
-            kept["gc"].wait_recv()
-        lo = n * (FF // 2)
-        whole = [s.gs[half].reshape(FF, TOK)[lo : lo + FF // 2] for half in range(2)]
         for place in range(4):
-            piece = s.xb[0, 0, place * 128 : (place + 1) * 128]
+            piece = jnp.concatenate(
+                [s.xb[q, 0, place * 128 : (place + 1) * 128] for q in range(4)], axis=1
+            )
             both = jnp.concatenate(
                 [dot(piece, whole[half], 1, 1).reshape(16, 8, FF // 2) for half in range(2)],
                 axis=1,
             ).reshape(4, 4, 16, FF // 2)
-            s.bw[n, place] = both
-            s.bg[n, place] = both.astype(BF)
+            if n == 0:
+                s.bw[n, place] = both
+                s.bg[n, place] = both.astype(BF)
+            else:
+                s.bw[n, :, place] = both
+                s.bg[n, :, place] = both.astype(BF)
 
     def base_out(n, task):
         grad = task.finish()
@@ -647,37 +681,40 @@
         o_ub[:, lo : lo + FF // 2] = grad[8:16]
 
     for n in range(2):
-        plan.add(f"bas{n}", lambda n=n: base_grads(n), [">gs1"] + ["bas0"] * n, 0.35)
+        plan.add(f"bas{n}", lambda n=n: base_grads(n), [f"ga{q}4" for q in range(4)], 0.7)
         bx = Scatter(
-            "dx",
-            lambda i, n=n: s.bg.at[n, (x + i) % 4],
-            lambda i, n=n: s.bw.at[n, (x + i) % 4],
+            ("dx", "dy")[n],
+            lambda i, n=n: s.bg.at[n, ((x, y)[n] + i) % 4],
+            lambda i, n=n: s.bw.at[n, ((x, y)[n] + i) % 4],
             lambda i, n=n: s.bxr.at[n, i],
             lambda i, n=n: s.bxf.at[n, i],
             rows(0, 2),
             rows(2, 4),
         )
         by = Direct(
-            "dy",
-            lambda i, n=n: s.by.at[n, (y + i) % 4],
-            lambda i, n=n: s.byw.at[n, (y + i) % 4],
+            ("dy", "dx")[n],
+            lambda i, n=n: s.by.at[n, ((y, x)[n] + i) % 4],
+            lambda i, n=n: s.byw.at[n, ((y, x)[n] + i) % 4],
             lambda i, n=n: s.byf.at[n, i],
         )
-        bz = Direct(
+        bz = Scatter(
             "dh",
             lambda i, n=n: s.bz.at[n, (h + i) % 4],
             lambda i, n=n: s.bzw.at[n, (h + i) % 4],
+            lambda i, n=n: s.bzr.at[n, i, :, 0 : (256, 128)[i]],
             lambda i, n=n: s.bzf.at[n, i],
+            lambda ref: ref.at[:, 0:256],
+            lambda ref: ref.at[:, 256:384],
         )
         scatter(
-            f"bx{n}", bx, "x", 0.375, [f"bas{n}"],
+            f"bx{n}", bx, ("x", "y")[n], 0.375, [f"bas{n}"],
             lambda n=n, bx=bx: keep(bx, s.byw.at[n], s.by.at[n]), 0.2,
         )
         direct(
-            f"by{n}", by, "y", 0.14, [f"bx{n}2"],
+            f"by{n}", by, ("y", "x")[n], 0.14, [f"bx{n}2"],
             lambda n=n, by=by: keep(by, s.bzw.at[n], s.bz.at[n]), 0.1,
         )
-        direct(f"bz{n}", bz, "z", 0.25, [f"by{n}2"], lambda n=n, bz=bz: base_out(n, bz), 0.1)
+        scatter(f"bz{n}", bz, "z", 0.1, [f"by{n}2"], lambda n=n, bz=bz: base_out(n, bz), 0.1)
 
     def weight_grads():
         for j in range(4):
@@ -732,20 +769,13 @@
         for n in range(2)
     ]
 
-    def base_input(n):
-        whole = [s.gs[half].reshape(FF, TOK) for half in range(2)]
-        lo = n * (FEAT // 2)
-        part = dot(gbase[lo : lo + 256], whole[0]) + dot(ubase[lo : lo + 256], whole[1])
-        s.dv[n, 0] = s.dv[n, 0] + part
-
     def token_out(n):
         lo = n * (FEAT // 2)
         o_tok[:, lo : lo + 256] = dh[n].finish().T.astype(BF)
 
     for n in range(2):
-        plan.add(f"bin{n}", lambda n=n: base_input(n), [">gs1", "bas0", f"d{n}y02"], 0.3)
         ring_h(f"d{n}h", dh[n], 0.5, lambda: None, 0.2)
-        plan.add(f"tok{n}", lambda n=n: token_out(n), [f"d{n}h2", f"bin{n}"], 0.2)
+        plan.add(f"tok{n}", lambda n=n: token_out(n), [f"d{n}h2"], 0.2)
 
     for name in plan.order():
         plan.steps[name][0]()
@@ -773,10 +803,10 @@
     outs = pl.pallas_call(
         kernel,
         out_shape=[jax.ShapeDtypeStruct(*shape) for shape in shapes],
-        in_specs=[vmem] * 2 + [anywhere] * 7,
+        in_specs=[anywhere] * 9,
         out_specs=[vmem] * 7,
         scratch_shapes=[pltpu.VMEM(*shape) for shape in SCRATCH.values()]
-        + [pltpu.SemaphoreType.DMA((SEMS,)), pltpu.SemaphoreType.DMA((SEMS,)), pltpu.SemaphoreType.DMA((7,))],
+        + [pltpu.SemaphoreType.DMA((SEMS,)), pltpu.SemaphoreType.DMA((SEMS,)), pltpu.SemaphoreType.DMA((9,))],
         compiler_params=pltpu.CompilerParams(
             collective_id=0, has_side_effects=True, vmem_limit_bytes=60 * 1024 * 1024
         ),

time: 155 us -> 152 us (0.981)
  Pallas kernels: 153 us -> 150 us
    pallas_call x1, Pallas kernels: 151 us -> 148 us  [local(): pl.pallas_call(kernel, out_shape=[jax.ShapeDtypeStruct(*shape) for shape...]
where the time goes in v3:
time: 152 us; the launch traced here: 151 us
  Pallas kernels  150 us (99%)
    pallas_call x1, Pallas kernels, local(): pl.pallas_call(kernel, out_shape=[jax.ShapeDtypeStruct(*shape) for shape...  148 us

profile of v3, /device:TPU:6, one launch (start us, length us, event | category | flops | bytes accessed | tf_op | source)
XLA Modules:
  0.0 150.8 jit_solution(7452816347414931385)
XLA Ops:
  0.6 148.1 %shard_map.144 = (bf16[128,512]{1,0:T(8,128)(2,1)}, f32[8,768]{1,0:T(8,128)}, f32[8,768]{1,0:T(8,128)}, f32[1,512,128]{2,1,0:T(8,128)}, f32[1,512,128]{2,1,0:T(8...) custom-call(bf16[128,512]{1,0:T(8,128)(2,1)} %refs_0_.1, s32[8,128]{1,0:T(8,128)} %bitcast.9, ...), custom_call_target="tpu_custom_call" | custom-call | tf_op jit(solution)/shard_map/pallas_call | solution.py:803
  148.8 2.0 %shard_map.145 = (bf16[128,512]{1,0:T(8,128)(2,1)}, f32[8,768]{1,0:T(8,128)}, f32[8,768]{1,0:T(8,128)}, f32[1,512,128]{2,1,0:T(8,128)}, f32[1,512,128]{2,1,0:T(8...) custom-call(bf16[128,512]{1,0:T(8,128)(2,1)} %get-tuple-element.21.refs_0_, f32[8,768]{1,0:T(8,128)} %get-tuple-element.22.refs_1_, ...), custom_call_target="tpu_custom_call" | custom-call | tf_op jit(solution)/shard_map/pallas_call | solution.py:824

commit v4 on v3

--- a/solution.py
+++ b/solution.py
@@ -92,14 +92,14 @@
 
 
 ORDER = (
-    0, 20, 15, 16, 21, 22, 3, 4, 40, 17, 5, 48, 1, 9, 18, 19, 49, 50, 6, 51, 23, 24, 10, 11, 108, 109, 110, 2, 12,
-    111, 52, 39, 44, 13, 27, 41, 25, 53, 33, 14, 138, 139, 140, 30, 141, 112, 31, 7, 8, 42, 45, 78, 79, 80, 47, 81,
-    28, 26, 54, 36, 142, 113, 34, 55, 29, 56, 57, 63, 64, 43, 114, 82, 65, 58, 143, 37, 35, 115, 116, 123, 124, 117,
-    118, 46, 66, 144, 83, 59, 32, 125, 38, 145, 146, 147, 153, 154, 67, 119, 148, 84, 60, 85, 126, 86, 87, 93, 94,
-    155, 120, 149, 88, 61, 127, 95, 156, 121, 150, 89, 62, 74, 122, 130, 134, 131, 157, 75, 96, 151, 135, 90, 128,
-    70, 71, 152, 160, 161, 164, 165, 68, 158, 97, 136, 162, 91, 166, 92, 100, 101, 129, 137, 159, 132, 69, 98, 163,
-    190, 104, 105, 167, 194, 102, 99, 168, 169, 177, 178, 133, 103, 106, 191, 186, 170, 187, 179, 107, 195, 171,
-    172, 180, 181, 76, 188, 173, 174, 72, 182, 183, 175, 184, 77, 196, 197, 73, 192, 193, 176, 189, 185,
+    0, 3, 15, 16, 20, 21, 22, 4, 40, 5, 48, 17, 18, 1, 6, 19, 49, 50, 9, 51, 7, 23, 24, 8, 78, 79, 80, 2, 12, 52,
+    81, 39, 44, 41, 13, 10, 25, 30, 53, 14, 31, 138, 82, 139, 11, 33, 140, 141, 27, 32, 108, 109, 34, 110, 42, 111,
+    28, 45, 26, 83, 47, 54, 142, 36, 55, 29, 56, 57, 63, 64, 43, 84, 65, 143, 112, 37, 58, 85, 86, 93, 94, 87, 88,
+    46, 66, 144, 113, 95, 59, 145, 38, 146, 147, 67, 153, 154, 89, 148, 114, 60, 35, 115, 116, 96, 155, 117, 123,
+    124, 90, 149, 118, 97, 61, 156, 91, 150, 119, 125, 62, 92, 100, 101, 74, 75, 157, 104, 70, 105, 126, 71, 76,
+    151, 120, 68, 102, 152, 164, 165, 158, 127, 160, 161, 69, 77, 98, 166, 121, 162, 122, 134, 135, 99, 130, 131,
+    106, 159, 128, 167, 194, 163, 190, 136, 129, 168, 169, 177, 178, 107, 132, 137, 195, 103, 170, 179, 72, 186,
+    187, 133, 191, 171, 172, 180, 181, 196, 197, 73, 188, 173, 174, 182, 183, 192, 193, 175, 189, 184, 176, 185,
 )
 
 

time: 152 us -> 145 us (0.954)
  Pallas kernels: 150 us -> 144 us
    pallas_call x1, Pallas kernels: 148 us -> 142 us  [local(): pl.pallas_call(kernel, out_shape=[jax.ShapeDtypeStruct(*shape) for shape...]
where the time goes in v4:
time: 145 us
  Pallas kernels  144 us (99%)
    pallas_call x1, Pallas kernels, local(): pl.pallas_call(kernel, out_shape=[jax.ShapeDtypeStruct(*shape) for shape...  142 us

profile of v4, /device:TPU:6, one launch (start us, length us, event | category | flops | bytes accessed | tf_op | source)
XLA Modules:
  0.0 144.7 jit_solution(11138168683402606571)
XLA Ops:
  0.6 142.0 %shard_map.144 = (bf16[128,512]{1,0:T(8,128)(2,1)}, f32[8,768]{1,0:T(8,128)}, f32[8,768]{1,0:T(8,128)}, f32[1,512,128]{2,1,0:T(8,128)}, f32[1,512,128]{2,1,0:T(8...) custom-call(bf16[128,512]{1,0:T(8,128)(2,1)} %refs_0_.1, s32[8,128]{1,0:T(8,128)} %bitcast.9, ...), custom_call_target="tpu_custom_call" | custom-call | tf_op jit(solution)/shard_map/pallas_call | solution.py:803
  142.7 2.0 %shard_map.145 = (bf16[128,512]{1,0:T(8,128)(2,1)}, f32[8,768]{1,0:T(8,128)}, f32[8,768]{1,0:T(8,128)}, f32[1,512,128]{2,1,0:T(8,128)}, f32[1,512,128]{2,1,0:T(8...) custom-call(bf16[128,512]{1,0:T(8,128)(2,1)} %get-tuple-element.21.refs_0_, f32[8,768]{1,0:T(8,128)} %get-tuple-element.22.refs_1_, ...), custom_call_target="tpu_custom_call" | custom-call | tf_op jit(solution)/shard_map/pallas_call | solution.py:824
